TPU v7x, 512 devices: a whole 4x4x16 slice. The times are simulated.
512 devices in a mesh: seq: 64 (over x_lo, z, core), head: 8 (over x_hi, y).
Axes of the slice: x: 4 (x_hi: 2, x_lo: 2; x = x_hi * 2 + x_lo), y: 4, z: 16, core: 2. Of those that a mesh axis runs over, the one named last changes fastest.
Arguments:
- query_in: bfloat16 [8192, 5120], P('seq', 'head'), may hold values from -8 to 8
- key_in: bfloat16 [8192, 5120], P('seq', 'head'), may hold values from -8 to 8
- value_in: bfloat16 [8192, 5120], P('seq', 'head'), may hold values from -6 to 6
- grad_out: bfloat16 [8192, 5120], P('seq', 'head'), may hold values from -6 to 6
- offsets: int32 [5, 40], P(None, 'head'), may hold values from 0 to 15, as said below
Outputs:
- attended: bfloat16 [8192, 5120], P('seq', 'head')
- log_norm: float32 [40, 8192], P('head', 'seq')
- grad_query: bfloat16 [8192, 5120], P('seq', 'head')
- grad_key: bfloat16 [8192, 5120], P('seq', 'head')
- grad_value: bfloat16 [8192, 5120], P('seq', 'head')
Inputs may be any that keep to these rules, and one draw needn't show every extreme that they name: offsets[l, h] is below 2^l for level l counted from 0; at the last level some head has offset 2^(4) - 1.
All inputs are finite; a program needn't handle non-finite values.
Results may differ from a plain program's by a relative error of at most 0.034.
Values may be sent and summed in bfloat16 or wider, within the bound.
A program may use at most 128 MiB of HBM per device.

v0:
```python
from functools import reduce

import jax
import jax.numpy as jnp
import numpy as np
from jax import lax
from jax.sharding import PartitionSpec as P

SUB = 512


masked_score = -1e30


def swapped(value, axis, distance):
    mask = 2**distance
    pairs = [(source, source ^ mask) for source in range(lax.axis_size(axis))]
    return lax.ppermute(value, axis, pairs)


def phase_mask(offset_row, dilation, extra_dims):
    matches = jnp.arange(dilation, dtype=jnp.int32)[None, :] == offset_row[:, None]
    return matches.reshape((offset_row.shape[0], 1, dilation) + (1,) * extra_dims)


def select_rows(source, offset_row, dilation):
    heads_here = source.shape[0]
    row_count = source.shape[1] // dilation
    reshaped = source.reshape((heads_here, row_count, dilation) + source.shape[2:])
    matches = phase_mask(offset_row, dilation, source.ndim - 2)
    zero = jnp.zeros((), source.dtype)
    return jnp.sum(jnp.where(matches, reshaped, zero), axis=2, dtype=source.dtype)


def spread_rows(source, offset_row, dilation, filler):
    heads_here = source.shape[0]
    row_count = source.shape[1]
    matches = phase_mask(offset_row, dilation, source.ndim - 2)
    widened = jnp.where(matches, source[:, :, None], filler)
    return widened.reshape((heads_here, row_count * dilation) + source.shape[2:])


def slot_index(bit_list, group_size, row_count):
    slot_table = np.zeros(group_size * row_count, np.int32)
    for slot_id in range(group_size):
        device_id = 0
        for place_id, bit_id in enumerate(bit_list):
            if slot_id >> place_id & 1:
                device_id += 1 << bit_id
        slot_table[slot_id * row_count : (slot_id + 1) * row_count] = (
            device_id * row_count + np.arange(row_count)
        )
    return jnp.asarray(slot_table)


def segment_mask(later, earlier):
    return (earlier[None, :] <= later[:, None]) & (earlier[None, :] // SUB == later[:, None] // SUB)


def swap_pairs(stacked, bit_id):
    return swapped(stacked, "seq", bit_id)


def swap_queries(stacked, bit_id):
    return swapped(stacked, "seq", bit_id)


def swap_stats(stacked, bit_id):
    return swapped(stacked, "seq", bit_id)


def double_up(stacked, bit_list, my_index, swapper):
    for bit_id in bit_list:
        partner = swapper(stacked, bit_id)
        is_upper = my_index >> bit_id & 1 == 1
        stacked = jnp.concatenate(
            [jnp.where(is_upper, partner, stacked), jnp.where(is_upper, stacked, partner)], axis=2
        )
    return stacked


def level_scores(query_rows, key_rows, allowed, score_scale):
    scores = (
        jnp.einsum("hqd,hkd->hqk", query_rows, key_rows, preferred_element_type=jnp.float32)
        * score_scale
    )
    return jnp.where(allowed[None], scores, masked_score)


def heads_first(flat_rows, heads_here):
    tokens = flat_rows.shape[0]
    head_size = flat_rows.shape[1] // heads_here
    return jnp.transpose(flat_rows.reshape(tokens, heads_here, head_size), (1, 0, 2))


def rows_first(per_head):
    heads_here, tokens, head_size = per_head.shape
    return jnp.transpose(per_head, (1, 0, 2)).reshape(tokens, heads_here * head_size)


def on_device(query_in, key_in, value_in, grad_out, offsets):
    levels_here = offsets.shape[0]
    heads_here = offsets.shape[1]
    tokens = query_in.shape[0]
    head_size = query_in.shape[1] // heads_here
    queries = heads_first(query_in, heads_here)
    keys_all = heads_first(key_in, heads_here)
    values_all = heads_first(value_in, heads_here)
    grads_all = heads_first(grad_out, heads_here)
    score_scale = head_size ** (-0.5)
    my_index = lax.axis_index("seq")
    saved_levels = []
    for level_id in range(levels_here):
        dilation = 2**level_id
        row_count = tokens // dilation
        group_size = max(1, SUB * dilation // tokens)
        bit_list = list(range(group_size.bit_length() - 1))
        offset_row = offsets[level_id]
        query_sub = select_rows(queries, offset_row, dilation)
        pair_sub = jnp.stack(
            [
                select_rows(keys_all, offset_row, dilation),
                select_rows(values_all, offset_row, dilation),
            ]
        )
        pair_group = double_up(pair_sub, bit_list, my_index, swap_pairs)
        key_index = slot_index(bit_list, group_size, row_count)
        query_index = my_index % group_size * row_count + jnp.arange(row_count, dtype=jnp.int32)
        allowed = segment_mask(query_index, key_index)
        scores = level_scores(query_sub, pair_group[0], allowed, score_scale)
        row_max = jnp.max(scores, axis=-1)
        weights = jnp.exp(scores - row_max[:, :, None])
        row_total = jnp.sum(weights, axis=-1)
        weighted = jnp.einsum(
            "hqk,hkd->hqd",
            weights.astype(jnp.bfloat16),
            pair_group[1],
            preferred_element_type=jnp.float32,
        )
        saved_levels.append(
            {
                "offset_row": offset_row,
                "dilation": dilation,
                "bit_list": bit_list,
                "query_sub": query_sub,
                "pair_sub": pair_sub,
                "pair_group": pair_group,
                "key_index": key_index,
                "query_index": query_index,
                "allowed": allowed,
                "row_max": row_max,
                "row_total": row_total,
                "weighted": weighted,
            }
        )
    spread_max = [
        spread_rows(
            level_entry["row_max"], level_entry["offset_row"], level_entry["dilation"], masked_score
        )
        for level_entry in saved_levels
    ]
    overall = reduce(jnp.maximum, spread_max)
    sum_total = jnp.zeros_like(overall)
    for level_entry, level_max in zip(saved_levels, spread_max):
        sum_total = sum_total + spread_rows(
            level_entry["row_total"], level_entry["offset_row"], level_entry["dilation"], 0.0
        ) * jnp.exp(level_max - overall)
    log_total = overall + jnp.log(sum_total)
    combined = jnp.zeros((heads_here, tokens, head_size), jnp.float32)
    for level_entry in saved_levels:
        factor = jnp.exp(
            level_entry["row_max"]
            - select_rows(log_total, level_entry["offset_row"], level_entry["dilation"])
        )
        combined = combined + spread_rows(
            level_entry["weighted"] * factor[:, :, None],
            level_entry["offset_row"],
            level_entry["dilation"],
            0.0,
        )
    out_heads = combined.astype(jnp.bfloat16)
    delta_rows = jnp.sum(grads_all.astype(jnp.float32) * out_heads.astype(jnp.float32), axis=-1)
    query_grad = jnp.zeros((heads_here, tokens, head_size), jnp.float32)
    key_grad = jnp.zeros((heads_here, tokens, head_size), jnp.float32)
    value_grad = jnp.zeros((heads_here, tokens, head_size), jnp.float32)
    for level_entry in saved_levels:
        offset_row = level_entry["offset_row"]
        dilation = level_entry["dilation"]
        bit_list = level_entry["bit_list"]
        query_sub = level_entry["query_sub"]
        pair_sub = level_entry["pair_sub"]
        pair_group = level_entry["pair_group"]
        grad_sub = select_rows(grads_all, offset_row, dilation)
        lse_sub = select_rows(log_total, offset_row, dilation)
        delta_sub = select_rows(delta_rows, offset_row, dilation)
        scores = level_scores(query_sub, pair_group[0], level_entry["allowed"], score_scale)
        probabilities = jnp.exp(scores - lse_sub[:, :, None])
        prob_grad = jnp.einsum(
            "hqd,hkd->hqk", grad_sub, pair_group[1], preferred_element_type=jnp.float32
        )
        score_grad = (score_scale * probabilities * (prob_grad - delta_sub[:, :, None])).astype(
            jnp.bfloat16
        )
        query_part = jnp.einsum(
            "hqk,hkd->hqd", score_grad, pair_group[0], preferred_element_type=jnp.float32
        )
        query_grad = query_grad + spread_rows(query_part, offset_row, dilation, 0.0)
        query_group = double_up(jnp.stack([query_sub, grad_sub]), bit_list, my_index, swap_queries)
        stat_group = double_up(jnp.stack([lse_sub, delta_sub]), bit_list, my_index, swap_stats)
        back_allowed = segment_mask(level_entry["key_index"], level_entry["query_index"])
        scores_back = level_scores(query_group[0], pair_sub[0], back_allowed, score_scale)
        probs_back = jnp.exp(scores_back - stat_group[0][:, :, None])
        grad_back = jnp.einsum(
            "hqd,hkd->hqk", query_group[1], pair_sub[1], preferred_element_type=jnp.float32
        )
        score_back = (score_scale * probs_back * (grad_back - stat_group[1][:, :, None])).astype(
            jnp.bfloat16
        )
        key_part = jnp.einsum(
            "hqk,hqd->hkd", score_back, query_group[0], preferred_element_type=jnp.float32
        )
        value_part = jnp.einsum(
            "hqk,hqd->hkd",
            probs_back.astype(jnp.bfloat16),
            query_group[1],
            preferred_element_type=jnp.float32,
        )
        key_grad = key_grad + spread_rows(key_part, offset_row, dilation, 0.0)
        value_grad = value_grad + spread_rows(value_part, offset_row, dilation, 0.0)
    return (
        rows_first(out_heads),
        log_total,
        rows_first(query_grad.astype(jnp.bfloat16)),
        rows_first(key_grad.astype(jnp.bfloat16)),
        rows_first(value_grad.astype(jnp.bfloat16)),
    )


def solution(mesh):
    return jax.shard_map(
        on_device,
        mesh=mesh,
        in_specs=(
            P("seq", "head"),
            P("seq", "head"),
            P("seq", "head"),
            P("seq", "head"),
            P(None, "head"),
        ),
        out_specs=(
            P("seq", "head"),
            P("head", "seq"),
            P("seq", "head"),
            P("seq", "head"),
            P("seq", "head"),
        ),
        check_vma=False,
    )
```

profile of v0, /device:TPU:1, one launch (start us, length us, event | category | flops | bytes accessed | tf_op | source)
XLA Modules:
  0.0 721.2 jit_solution(5182916929292329375)
XLA Ops:
  5.3 8.8 %collective-permute-start.48 = (bf16[2,5,8,128]{3,2,1,0:T(8,128)(2,1)S(1)}, bf16[2,5,8,128]{3,2,1,0:T(8,128)(2,1)S(1)}, u32[]{:S(2)}, u32[]{:S(2)}) collective-permute-start(bf16[2,5,8,128]{3,2,1,0:T(8,128)(2,1)S(1)} %pad_maximum_fusion.49), channel_id=1, source_target_pairs={{0,8},{8,0},{16,24},{24,16},{32,40},{40,32},{48,56},{56,48},{64,72... | collective-permute-start | bytes 61448 | tf_op jit(solution)/shard_map/ppermute | solution.py:18
  14.1 1.9 collective-permute-start.14
  17.6 2.4 collective-permute-start
  22.6 2.4 collective-permute-start.9
  45.5 2.4 collective-permute-start.5
  48.0 1.9 collective-permute-start.24
  52.0 2.7 collective-permute-done.15
  56.7 2.8 collective-permute-done.49
  59.5 4.7 collective-permute-start.2
  68.2 3.1 collective-permute-done.10
  71.3 2.5 collective-permute-start.39
  73.9 2.6 collective-permute-done.39
  78.5 5.0 collective-permute-done.16
  85.4 4.5 collective-permute-done.50
  91.9 3.4 collective-permute-start.31
  95.3 1.9 collective-permute-start.11
  97.4 4.3 collective-permute-start.40
  101.8 5.2 collective-permute-start.17
  107.2 4.0 collective-permute-start.51
  111.3 5.7 collective-permute-done.40
  119.0 3.4 collective-permute-start.25
  122.5 2.5 collective-permute-done.51
  125.0 8.1 %collective-permute-start.7 = (bf16[2,5,128,128]{3,2,1,0:T(8,128)(2,1)S(1)}, bf16[2,5,128,128]{3,2,1,0:T(8,128)(2,1)S(1)}, u32[]{:S(2)}, u32[]{:S(2)}) collective-permute-start(bf16[2,5,128,128]{3,2,1,0:T(8,128)(2,1)S(1)} %pad_maximum_fusion.22), channel_id=1, source_target_pairs={{0,32},{8,40},{16,48},{24,56},{32,0},{40,8},{48,16},{56,24},{64,96... | collective-permute-start | bytes 983048 | tf_op jit(solution)/shard_map/ppermute | solution.py:18
  136.3 8.0 %collective-permute-start.12 = (bf16[2,5,128,128]{3,2,1,0:T(8,128)(2,1)S(1)}, bf16[2,5,128,128]{3,2,1,0:T(8,128)(2,1)S(1)}, u32[]{:S(2)}, u32[]{:S(2)}) collective-permute-start(bf16[2,5,128,128]{3,2,1,0:T(8,128)(2,1)S(1)} %pad_maximum_fusion.23), channel_id=1, source_target_pairs={{0,64},{8,72},{16,80},{24,88},{32,96},{40,104},{48,112},{56,120},{... | collective-permute-start | bytes 983048 | tf_op jit(solution)/shard_map/ppermute | solution.py:18
  145.3 4.6 collective-permute-start.41
  151.2 14.7 %collective-permute-start.18 = (bf16[2,5,128,128]{3,2,1,0:T(8,128)(2,1)S(1)}, bf16[2,5,128,128]{3,2,1,0:T(8,128)(2,1)S(1)}, u32[]{:S(2)}, u32[]{:S(2)}) collective-permute-start(bf16[2,5,128,128]{3,2,1,0:T(8,128)(2,1)S(1)} %pad_maximum_fusion.24), channel_id=1, source_target_pairs={{0,128},{8,136},{16,144},{24,152},{32,160},{40,168},{48,176},{56,1... | collective-permute-start | bytes 983048 | tf_op jit(solution)/shard_map/ppermute | solution.py:18
  170.2 32.2 %collective-permute-start.1 = (bf16[2,5,256,128]{3,2,1,0:T(8,128)(2,1)S(1)}, bf16[2,5,256,128]{3,2,1,0:T(8,128)(2,1)S(1)}, u32[]{:S(2)}, u32[]{:S(2)}) collective-permute-start(bf16[2,5,256,128]{3,2,1,0:T(8,128)(2,1)S(1)} %pad_maximum_fusion.10), channel_id=1, source_target_pairs={{0,16},{8,24},{16,0},{24,8},{32,48},{40,56},{48,32},{56,40},{64,80... | collective-permute-start | bytes 1966088 | tf_op jit(solution)/shard_map/ppermute | solution.py:18
  203.7 28.0 %collective-permute-start.21 = (bf16[2,5,256,128]{3,2,1,0:T(8,128)(2,1)}, bf16[2,5,256,128]{3,2,1,0:T(8,128)(2,1)}, u32[]{:S(2)}, u32[]{:S(2)}) collective-permute-start(bf16[2,5,256,128]{3,2,1,0:T(8,128)(2,1)} %pad_maximum_fusion.15), channel_id=1, source_target_pairs={{0,16},{8,24},{16,0},{24,8},{32,48},{40,56},{48,32},{56,40},{64,80... | collective-permute-start | bytes 1966088 | tf_op jit(solution)/shard_map/ppermute | solution.py:18
  232.9 5.9 collective-permute-start.4
  239.9 17.2 %collective-permute-start.26 = (bf16[2,5,256,128]{3,2,1,0:T(8,128)(2,1)}, bf16[2,5,256,128]{3,2,1,0:T(8,128)(2,1)}, u32[]{:S(2)}, u32[]{:S(2)}) collective-permute-start(bf16[2,5,256,128]{3,2,1,0:T(8,128)(2,1)} %pad_maximum_fusion.16), channel_id=1, source_target_pairs={{0,32},{8,40},{16,48},{24,56},{32,0},{40,8},{48,16},{56,24},{64,96... | collective-permute-start | bytes 1966088 | tf_op jit(solution)/shard_map/ppermute | solution.py:18
  261.4 26.7 %collective-permute-start.33 = (bf16[2,5,256,128]{3,2,1,0:T(8,128)(2,1)}, bf16[2,5,256,128]{3,2,1,0:T(8,128)(2,1)}, u32[]{:S(2)}, u32[]{:S(2)}) collective-permute-start(bf16[2,5,256,128]{3,2,1,0:T(8,128)(2,1)} %pad_maximum_fusion.17), channel_id=1, source_target_pairs={{0,64},{8,72},{16,80},{24,88},{32,96},{40,104},{48,112},{56,120},{... | collective-permute-start | bytes 1966088 | tf_op jit(solution)/shard_map/ppermute | solution.py:18
  295.9 18.5 %collective-permute-done.21 = bf16[2,5,256,128]{3,2,1,0:T(8,128)(2,1)} collective-permute-done((bf16[2,5,256,128]{3,2,1,0:T(8,128)(2,1)}, bf16[2,5,256,128]{3,2,1,0:T(8,128)(2,1)}, u32[]{:S(2)}, u32[]{:S(2)}) %collective-permute-start.21) | collective-permute-done | bytes 655392 | tf_op jit(solution)/shard_map/ppermute | solution.py:18
  314.4 12.0 %collective-permute-start.13 = (bf16[2,5,256,128]{3,2,1,0:T(8,128)(2,1)}, bf16[2,5,256,128]{3,2,1,0:T(8,128)(2,1)}, u32[]{:S(2)}, u32[]{:S(2)}) collective-permute-start(bf16[2,5,256,128]{3,2,1,0:T(8,128)(2,1)} %pad_maximum_fusion.13), channel_id=1, source_target_pairs={{0,128},{8,136},{16,144},{24,152},{32,160},{40,168},{48,176},{56,1... | collective-permute-start | bytes 1966088 | tf_op jit(solution)/shard_map/ppermute | solution.py:18
  326.4 2.6 broadcast_select_fusion.16
  329.0 2.0 collective-permute-start.42
  336.2 11.1 %collective-permute-start.19 = (bf16[2,5,256,128]{3,2,1,0:T(8,128)(2,1)}, bf16[2,5,256,128]{3,2,1,0:T(8,128)(2,1)}, u32[]{:S(2)}, u32[]{:S(2)}) collective-permute-start(bf16[2,5,256,128]{3,2,1,0:T(8,128)(2,1)} %pad_maximum_fusion.14), channel_id=1, source_target_pairs={{0,256},{8,264},{16,272},{24,280},{32,288},{40,296},{48,304},{56,3... | collective-permute-start | bytes 1966088 | tf_op jit(solution)/shard_map/ppermute | solution.py:18
  347.3 2.5 broadcast_select_fusion.12
  349.8 2.1 collective-permute-start.53
  354.9 2.5 broadcast_select_fusion.8
  367.3 2.6 broadcast_select_fusion.4
  376.8 2.0 select_reduce_fusion.13
  385.6 2.0 fusion.257
  400.6 2.2 fusion.222
  422.3 2.4 multiply_reduce_fusion
  439.7 31.3 %collective-permute-start.54 = (f32[2,5,8]{2,1,0:T(8,128)}, f32[2,5,8]{2,1,0:T(8,128)}, u32[]{:S(2)}, u32[]{:S(2)}) collective-permute-start(f32[2,5,8]{2,1,0:T(8,128)} %pad_maximum_fusion.68), channel_id=1, source_target_pairs={{0,8},{8,0},{16,24},{24,16},{32,40},{40,32},{48,56},{56,48},{64,72... | collective-permute-start | bytes 968 | tf_op jit(solution)/shard_map/ppermute | solution.py:18
  476.1 1.9 fusion.67
  484.6 2.4 collective-permute-start.34
  489.3 2.1 collective-permute-start.27
  493.5 2.5 fusion.53
  497.3 2.5 collective-permute-start.43
  499.9 2.5 broadcast_select_fusion.1
  503.8 121.5 %collective-permute-start.55 = (f32[2,5,16]{2,1,0:T(8,128)S(1)}, f32[2,5,16]{2,1,0:T(8,128)S(1)}, u32[]{:S(2)}, u32[]{:S(2)}) collective-permute-start(f32[2,5,16]{2,1,0:T(8,128)S(1)} %pad_maximum_fusion.69), channel_id=1, source_target_pairs={{0,16},{8,24},{16,0},{24,8},{32,48},{40,56},{48,32},{56,40},{64,80... | collective-permute-start | bytes 1928 | tf_op jit(solution)/shard_map/ppermute | solution.py:18
  627.6 8.5 %collective-permute-start.56 = (f32[2,5,32]{2,1,0:T(8,128)S(1)}, f32[2,5,32]{2,1,0:T(8,128)S(1)}, u32[]{:S(2)}, u32[]{:S(2)}) collective-permute-start(f32[2,5,32]{2,1,0:T(8,128)S(1)} %pad_maximum_fusion.70), channel_id=1, source_target_pairs={{0,32},{8,40},{16,48},{24,56},{32,0},{40,8},{48,16},{56,24},{64,96... | collective-permute-start | bytes 3848 | tf_op jit(solution)/shard_map/ppermute | solution.py:18
  636.9 3.4 collective-permute-start.35
  642.5 2.8 collective-permute-start.57
  646.1 3.4 collective-permute-start.28
  651.8 7.3 %collective-permute-start.46 = (f32[2,5,128]{2,1,0:T(8,128)S(1)}, f32[2,5,128]{2,1,0:T(8,128)S(1)}, u32[]{:S(2)}, u32[]{:S(2)}) collective-permute-start(f32[2,5,128]{2,1,0:T(8,128)S(1)} %pad_maximum_fusion.67), channel_id=1, source_target_pairs={{0,64},{8,72},{16,80},{24,88},{32,96},{40,104},{48,112},{56,120},{... | collective-permute-start | bytes 15368 | tf_op jit(solution)/shard_map/ppermute | solution.py:18
  659.2 5.8 collective-permute-start.58
  665.7 3.4 collective-permute-start.23
  671.2 6.4 collective-permute-start.37
  677.7 4.7 collective-permute-start.47
  682.4 3.1 collective-permute-start.59
  706.9 2.7 fusion.56
  713.6 3.0 fusion.55
  (729 shorter events, 208.2 us)
Async XLA Ops:
  5.3 38.3 %collective-permute-start.48 = (bf16[2,5,8,128]{3,2,1,0:T(8,128)(2,1)S(1)}, bf16[2,5,8,128]{3,2,1,0:T(8,128)(2,1)S(1)}, u32[]{:S(2)}, u32[]{:S(2)}) collective-permute-start(bf16[2,5,8,128]{3,2,1,0:T(8,128)(2,1)S(1)} %pad_maximum_fusion.49), channel_id=1, source_target_pairs={{0,8},{8,0},{16,24},{24,16},{32,40},{40,32},{48,56},{56,48},{64,72... | collective-permute-start | bytes 61448 | tf_op jit(solution)/shard_map/ppermute | solution.py:18
  14.1 31.4 %collective-permute-start.14 = (bf16[2,5,8,128]{3,2,1,0:T(8,128)(2,1)S(1)}, bf16[2,5,8,128]{3,2,1,0:T(8,128)(2,1)S(1)}, u32[]{:S(2)}, u32[]{:S(2)}) collective-permute-start(bf16[2,5,8,128]{3,2,1,0:T(8,128)(2,1)S(1)} %pad_maximum_fusion.48), channel_id=1, source_target_pairs={{0,8},{8,0},{16,24},{24,16},{32,40},{40,32},{48,56},{56,48},{64,72... | collective-permute-start | bytes 61448 | tf_op jit(solution)/shard_map/ppermute | solution.py:18
  16.8 271.7 %copy-start.126 = (pred[5]{0:T(512)(128)(4,1)}, pred[5]{0:T(512)(128)(4,1)S(1)}, u32[]{:S(2)}) copy-start(pred[5]{0:T(512)(128)(4,1)S(1)} %compare_bitcast_fusion) | copy-start | bytes 19
  17.6 115.6 %collective-permute-start = (bf16[2,5,128,128]{3,2,1,0:T(8,128)(2,1)}, bf16[2,5,128,128]{3,2,1,0:T(8,128)(2,1)}, u32[]{:S(2)}, u32[]{:S(2)}) collective-permute-start(bf16[2,5,128,128]{3,2,1,0:T(8,128)(2,1)} %pad_maximum_fusion.20), channel_id=1, source_target_pairs={{0,8},{8,0},{16,24},{24,16},{32,40},{40,32},{48,56},{56,48},{64,72... | collective-permute-start | bytes 983048 | tf_op jit(solution)/shard_map/ppermute | solution.py:18
  20.7 27.4 %collective-permute-start.38 = (bf16[2,5,16,128]{3,2,1,0:T(8,128)(2,1)S(1)}, bf16[2,5,16,128]{3,2,1,0:T(8,128)(2,1)S(1)}, u32[]{:S(2)}, u32[]{:S(2)}) collective-permute-start(bf16[2,5,16,128]{3,2,1,0:T(8,128)(2,1)S(1)} %pad_maximum_fusion.46), channel_id=1, source_target_pairs={{0,8},{8,0},{16,24},{24,16},{32,40},{40,32},{48,56},{56,48},{64,72... | collective-permute-start | bytes 122888 | tf_op jit(solution)/shard_map/ppermute | solution.py:18
  22.6 27.3 %collective-permute-start.9 = (bf16[2,5,16,128]{3,2,1,0:T(8,128)(2,1)S(1)}, bf16[2,5,16,128]{3,2,1,0:T(8,128)(2,1)S(1)}, u32[]{:S(2)}, u32[]{:S(2)}) collective-permute-start(bf16[2,5,16,128]{3,2,1,0:T(8,128)(2,1)S(1)} %pad_maximum_fusion.44), channel_id=1, source_target_pairs={{0,8},{8,0},{16,24},{24,16},{32,40},{40,32},{48,56},{56,48},{64,72... | collective-permute-start | bytes 122888 | tf_op jit(solution)/shard_map/ppermute | solution.py:18
  43.6 20.6 %collective-permute-start.30 = (bf16[2,5,32,128]{3,2,1,0:T(8,128)(2,1)S(1)}, bf16[2,5,32,128]{3,2,1,0:T(8,128)(2,1)S(1)}, u32[]{:S(2)}, u32[]{:S(2)}) collective-permute-start(bf16[2,5,32,128]{3,2,1,0:T(8,128)(2,1)S(1)} %pad_maximum_fusion.41), channel_id=1, source_target_pairs={{0,8},{8,0},{16,24},{24,16},{32,40},{40,32},{48,56},{56,48},{64,72... | collective-permute-start | bytes 245768 | tf_op jit(solution)/shard_map/ppermute | solution.py:18
  45.5 20.6 %collective-permute-start.5 = (bf16[2,5,32,128]{3,2,1,0:T(8,128)(2,1)S(1)}, bf16[2,5,32,128]{3,2,1,0:T(8,128)(2,1)S(1)}, u32[]{:S(2)}, u32[]{:S(2)}) collective-permute-start(bf16[2,5,32,128]{3,2,1,0:T(8,128)(2,1)S(1)} %pad_maximum_fusion.38), channel_id=1, source_target_pairs={{0,8},{8,0},{16,24},{24,16},{32,40},{40,32},{48,56},{56,48},{64,72... | collective-permute-start | bytes 245768 | tf_op jit(solution)/shard_map/ppermute | solution.py:18
  48.0 43.9 %collective-permute-start.24 = (bf16[2,5,64,128]{3,2,1,0:T(8,128)(2,1)S(1)}, bf16[2,5,64,128]{3,2,1,0:T(8,128)(2,1)S(1)}, u32[]{:S(2)}, u32[]{:S(2)}) collective-permute-start(bf16[2,5,64,128]{3,2,1,0:T(8,128)(2,1)S(1)} %pad_maximum_fusion.34), channel_id=1, source_target_pairs={{0,8},{8,0},{16,24},{24,16},{32,40},{40,32},{48,56},{56,48},{64,72... | collective-permute-start | bytes 491528 | tf_op jit(solution)/shard_map/ppermute | solution.py:18
  50.0 4.7 collective-permute-start.15
  54.7 4.7 collective-permute-start.49
  59.5 35.8 %collective-permute-start.2 = (bf16[2,5,64,128]{3,2,1,0:T(8,128)(2,1)S(1)}, bf16[2,5,64,128]{3,2,1,0:T(8,128)(2,1)S(1)}, u32[]{:S(2)}, u32[]{:S(2)}) collective-permute-start(bf16[2,5,64,128]{3,2,1,0:T(8,128)(2,1)S(1)} %pad_maximum_fusion.30), channel_id=1, source_target_pairs={{0,8},{8,0},{16,24},{24,16},{32,40},{40,32},{48,56},{56,48},{64,72... | collective-permute-start | bytes 491528 | tf_op jit(solution)/shard_map/ppermute | solution.py:18
  64.2 72.0 %collective-permute-start.20 = (bf16[2,5,128,128]{3,2,1,0:T(8,128)(2,1)}, bf16[2,5,128,128]{3,2,1,0:T(8,128)(2,1)S(1)}, u32[]{:S(2)}, u32[]{:S(2)}) collective-permute-start(bf16[2,5,128,128]{3,2,1,0:T(8,128)(2,1)} %pad_maximum_fusion.25), channel_id=1, source_target_pairs={{0,8},{8,0},{16,24},{24,16},{32,40},{40,32},{48,56},{56,48},{64,72... | collective-permute-start | bytes 983048 | tf_op jit(solution)/shard_map/ppermute | solution.py:18
  66.2 5.2 collective-permute-start.10
  71.3 5.2 collective-permute-start.39
  76.5 7.0 collective-permute-start.16
  83.5 6.4 collective-permute-start.50
  89.9 7.5 %collective-permute-start.6 = (bf16[2,5,64,128]{3,2,1,0:T(8,128)(2,1)S(1)}, bf16[2,5,64,128]{3,2,1,0:T(8,128)(2,1)S(1)}, u32[]{:S(2)}, u32[]{:S(2)}) collective-permute-start(bf16[2,5,64,128]{3,2,1,0:T(8,128)(2,1)S(1)} %pad_maximum_fusion.31), channel_id=1, source_target_pairs={{0,16},{8,24},{16,0},{24,8},{32,48},{40,56},{48,32},{56,40},{64,80... | collective-permute-start | bytes 491528 | tf_op jit(solution)/shard_map/ppermute | solution.py:18
  91.9 9.9 %collective-permute-start.31 = (bf16[2,5,64,128]{3,2,1,0:T(8,128)(2,1)S(1)}, bf16[2,5,64,128]{3,2,1,0:T(8,128)(2,1)S(1)}, u32[]{:S(2)}, u32[]{:S(2)}) collective-permute-start(bf16[2,5,64,128]{3,2,1,0:T(8,128)(2,1)S(1)} %pad_maximum_fusion.35), channel_id=1, source_target_pairs={{0,16},{8,24},{16,0},{24,8},{32,48},{40,56},{48,32},{56,40},{64,80... | collective-permute-start | bytes 491528 | tf_op jit(solution)/shard_map/ppermute | solution.py:18
  95.3 11.8 %collective-permute-start.11 = (bf16[2,5,64,128]{3,2,1,0:T(8,128)(2,1)S(1)}, bf16[2,5,64,128]{3,2,1,0:T(8,128)(2,1)S(1)}, u32[]{:S(2)}, u32[]{:S(2)}) collective-permute-start(bf16[2,5,64,128]{3,2,1,0:T(8,128)(2,1)S(1)} %pad_maximum_fusion.32), channel_id=1, source_target_pairs={{0,32},{8,40},{16,48},{24,56},{32,0},{40,8},{48,16},{56,24},{64,96... | collective-permute-start | bytes 491528 | tf_op jit(solution)/shard_map/ppermute | solution.py:18
  97.4 19.5 %collective-permute-start.40 = (bf16[2,5,64,128]{3,2,1,0:T(8,128)(2,1)S(1)}, bf16[2,5,64,128]{3,2,1,0:T(8,128)(2,1)S(1)}, u32[]{:S(2)}, u32[]{:S(2)}) collective-permute-start(bf16[2,5,64,128]{3,2,1,0:T(8,128)(2,1)S(1)} %pad_maximum_fusion.36), channel_id=1, source_target_pairs={{0,32},{8,40},{16,48},{24,56},{32,0},{40,8},{48,16},{56,24},{64,96... | collective-permute-start | bytes 491528 | tf_op jit(solution)/shard_map/ppermute | solution.py:18
  101.8 17.2 %collective-permute-start.17 = (bf16[2,5,64,128]{3,2,1,0:T(8,128)(2,1)S(1)}, bf16[2,5,64,128]{3,2,1,0:T(8,128)(2,1)S(1)}, u32[]{:S(2)}, u32[]{:S(2)}) collective-permute-start(bf16[2,5,64,128]{3,2,1,0:T(8,128)(2,1)S(1)} %pad_maximum_fusion.33), channel_id=1, source_target_pairs={{0,64},{8,72},{16,80},{24,88},{32,96},{40,104},{48,112},{56,120},{... | collective-permute-start | bytes 491528 | tf_op jit(solution)/shard_map/ppermute | solution.py:18
  107.2 17.8 %collective-permute-start.51 = (bf16[2,5,64,128]{3,2,1,0:T(8,128)(2,1)S(1)}, bf16[2,5,64,128]{3,2,1,0:T(8,128)(2,1)S(1)}, u32[]{:S(2)}, u32[]{:S(2)}) collective-permute-start(bf16[2,5,64,128]{3,2,1,0:T(8,128)(2,1)S(1)} %pad_maximum_fusion.37), channel_id=1, source_target_pairs={{0,64},{8,72},{16,80},{24,88},{32,96},{40,104},{48,112},{56,120},{... | collective-permute-start | bytes 491528 | tf_op jit(solution)/shard_map/ppermute | solution.py:18
  116.9 28.4 %collective-permute-start.3 = (bf16[2,5,128,128]{3,2,1,0:T(8,128)(2,1)S(1)}, bf16[2,5,128,128]{3,2,1,0:T(8,128)(2,1)S(1)}, u32[]{:S(2)}, u32[]{:S(2)}) collective-permute-start(bf16[2,5,128,128]{3,2,1,0:T(8,128)(2,1)S(1)} %pad_maximum_fusion.21), channel_id=1, source_target_pairs={{0,16},{8,24},{16,0},{24,8},{32,48},{40,56},{48,32},{56,40},{64,80... | collective-permute-start | bytes 983048 | tf_op jit(solution)/shard_map/ppermute | solution.py:18
  119.0 32.1 %collective-permute-start.25 = (bf16[2,5,128,128]{3,2,1,0:T(8,128)(2,1)S(1)}, bf16[2,5,128,128]{3,2,1,0:T(8,128)(2,1)S(1)}, u32[]{:S(2)}, u32[]{:S(2)}) collective-permute-start(bf16[2,5,128,128]{3,2,1,0:T(8,128)(2,1)S(1)} %pad_maximum_fusion.26), channel_id=1, source_target_pairs={{0,16},{8,24},{16,0},{24,8},{32,48},{40,56},{48,32},{56,40},{64,80... | collective-permute-start | bytes 983048 | tf_op jit(solution)/shard_map/ppermute | solution.py:18
  125.0 42.2 %collective-permute-start.7 = (bf16[2,5,128,128]{3,2,1,0:T(8,128)(2,1)S(1)}, bf16[2,5,128,128]{3,2,1,0:T(8,128)(2,1)S(1)}, u32[]{:S(2)}, u32[]{:S(2)}) collective-permute-start(bf16[2,5,128,128]{3,2,1,0:T(8,128)(2,1)S(1)} %pad_maximum_fusion.22), channel_id=1, source_target_pairs={{0,32},{8,40},{16,48},{24,56},{32,0},{40,8},{48,16},{56,24},{64,96... | collective-permute-start | bytes 983048 | tf_op jit(solution)/shard_map/ppermute | solution.py:18
  133.3 37.0 %collective-permute-start.32 = (bf16[2,5,128,128]{3,2,1,0:T(8,128)(2,1)S(1)}, bf16[2,5,128,128]{3,2,1,0:T(8,128)(2,1)S(1)}, u32[]{:S(2)}, u32[]{:S(2)}) collective-permute-start(bf16[2,5,128,128]{3,2,1,0:T(8,128)(2,1)S(1)} %pad_maximum_fusion.27), channel_id=1, source_target_pairs={{0,32},{8,40},{16,48},{24,56},{32,0},{40,8},{48,16},{56,24},{64,96... | collective-permute-start | bytes 983048 | tf_op jit(solution)/shard_map/ppermute | solution.py:18
  136.3 67.3 %collective-permute-start.12 = (bf16[2,5,128,128]{3,2,1,0:T(8,128)(2,1)S(1)}, bf16[2,5,128,128]{3,2,1,0:T(8,128)(2,1)S(1)}, u32[]{:S(2)}, u32[]{:S(2)}) collective-permute-start(bf16[2,5,128,128]{3,2,1,0:T(8,128)(2,1)S(1)} %pad_maximum_fusion.23), channel_id=1, source_target_pairs={{0,64},{8,72},{16,80},{24,88},{32,96},{40,104},{48,112},{56,120},{... | collective-permute-start | bytes 983048 | tf_op jit(solution)/shard_map/ppermute | solution.py:18
  145.3 87.5 %collective-permute-start.41 = (bf16[2,5,128,128]{3,2,1,0:T(8,128)(2,1)S(1)}, bf16[2,5,128,128]{3,2,1,0:T(8,128)(2,1)S(1)}, u32[]{:S(2)}, u32[]{:S(2)}) collective-permute-start(bf16[2,5,128,128]{3,2,1,0:T(8,128)(2,1)S(1)} %pad_maximum_fusion.28), channel_id=1, source_target_pairs={{0,64},{8,72},{16,80},{24,88},{32,96},{40,104},{48,112},{56,120},{... | collective-permute-start | bytes 983048 | tf_op jit(solution)/shard_map/ppermute | solution.py:18
  151.2 88.7 %collective-permute-start.18 = (bf16[2,5,128,128]{3,2,1,0:T(8,128)(2,1)S(1)}, bf16[2,5,128,128]{3,2,1,0:T(8,128)(2,1)S(1)}, u32[]{:S(2)}, u32[]{:S(2)}) collective-permute-start(bf16[2,5,128,128]{3,2,1,0:T(8,128)(2,1)S(1)} %pad_maximum_fusion.24), channel_id=1, source_target_pairs={{0,128},{8,136},{16,144},{24,152},{32,160},{40,168},{48,176},{56,1... | collective-permute-start | bytes 983048 | tf_op jit(solution)/shard_map/ppermute | solution.py:18
  167.2 91.2 %collective-permute-start.52 = (bf16[2,5,128,128]{3,2,1,0:T(8,128)(2,1)S(1)}, bf16[2,5,128,128]{3,2,1,0:T(8,128)(2,1)S(1)}, u32[]{:S(2)}, u32[]{:S(2)}) collective-permute-start(bf16[2,5,128,128]{3,2,1,0:T(8,128)(2,1)S(1)} %pad_maximum_fusion.29), channel_id=1, source_target_pairs={{0,128},{8,136},{16,144},{24,152},{32,160},{40,168},{48,176},{56,1... | collective-permute-start | bytes 983048 | tf_op jit(solution)/shard_map/ppermute | solution.py:18
  170.2 91.2 %collective-permute-start.1 = (bf16[2,5,256,128]{3,2,1,0:T(8,128)(2,1)S(1)}, bf16[2,5,256,128]{3,2,1,0:T(8,128)(2,1)S(1)}, u32[]{:S(2)}, u32[]{:S(2)}) collective-permute-start(bf16[2,5,256,128]{3,2,1,0:T(8,128)(2,1)S(1)} %pad_maximum_fusion.10), channel_id=1, source_target_pairs={{0,16},{8,24},{16,0},{24,8},{32,48},{40,56},{48,32},{56,40},{64,80... | collective-permute-start | bytes 1966088 | tf_op jit(solution)/shard_map/ppermute | solution.py:18
  203.7 110.7 %collective-permute-start.21 = (bf16[2,5,256,128]{3,2,1,0:T(8,128)(2,1)}, bf16[2,5,256,128]{3,2,1,0:T(8,128)(2,1)}, u32[]{:S(2)}, u32[]{:S(2)}) collective-permute-start(bf16[2,5,256,128]{3,2,1,0:T(8,128)(2,1)} %pad_maximum_fusion.15), channel_id=1, source_target_pairs={{0,16},{8,24},{16,0},{24,8},{32,48},{40,56},{48,32},{56,40},{64,80... | collective-permute-start | bytes 1966088 | tf_op jit(solution)/shard_map/ppermute | solution.py:18
  232.9 96.1 %collective-permute-start.4 = (bf16[2,5,256,128]{3,2,1,0:T(8,128)(2,1)}, bf16[2,5,256,128]{3,2,1,0:T(8,128)(2,1)}, u32[]{:S(2)}, u32[]{:S(2)}) collective-permute-start(bf16[2,5,256,128]{3,2,1,0:T(8,128)(2,1)} %pad_maximum_fusion.11), channel_id=1, source_target_pairs={{0,32},{8,40},{16,48},{24,56},{32,0},{40,8},{48,16},{56,24},{64,96... | collective-permute-start | bytes 1966088 | tf_op jit(solution)/shard_map/ppermute | solution.py:18
  239.9 96.3 %collective-permute-start.26 = (bf16[2,5,256,128]{3,2,1,0:T(8,128)(2,1)}, bf16[2,5,256,128]{3,2,1,0:T(8,128)(2,1)}, u32[]{:S(2)}, u32[]{:S(2)}) collective-permute-start(bf16[2,5,256,128]{3,2,1,0:T(8,128)(2,1)} %pad_maximum_fusion.16), channel_id=1, source_target_pairs={{0,32},{8,40},{16,48},{24,56},{32,0},{40,8},{48,16},{56,24},{64,96... | collective-permute-start | bytes 1966088 | tf_op jit(solution)/shard_map/ppermute | solution.py:18
  258.3 91.5 %collective-permute-start.8 = (bf16[2,5,256,128]{3,2,1,0:T(8,128)(2,1)}, bf16[2,5,256,128]{3,2,1,0:T(8,128)(2,1)}, u32[]{:S(2)}, u32[]{:S(2)}) collective-permute-start(bf16[2,5,256,128]{3,2,1,0:T(8,128)(2,1)} %pad_maximum_fusion.12), channel_id=1, source_target_pairs={{0,64},{8,72},{16,80},{24,88},{32,96},{40,104},{48,112},{56,120},{... | collective-permute-start | bytes 1966088 | tf_op jit(solution)/shard_map/ppermute | solution.py:18
  261.4 92.4 %collective-permute-start.33 = (bf16[2,5,256,128]{3,2,1,0:T(8,128)(2,1)}, bf16[2,5,256,128]{3,2,1,0:T(8,128)(2,1)}, u32[]{:S(2)}, u32[]{:S(2)}) collective-permute-start(bf16[2,5,256,128]{3,2,1,0:T(8,128)(2,1)} %pad_maximum_fusion.17), channel_id=1, source_target_pairs={{0,64},{8,72},{16,80},{24,88},{32,96},{40,104},{48,112},{56,120},{... | collective-permute-start | bytes 1966088 | tf_op jit(solution)/shard_map/ppermute | solution.py:18
  314.4 46.3 %collective-permute-start.13 = (bf16[2,5,256,128]{3,2,1,0:T(8,128)(2,1)}, bf16[2,5,256,128]{3,2,1,0:T(8,128)(2,1)}, u32[]{:S(2)}, u32[]{:S(2)}) collective-permute-start(bf16[2,5,256,128]{3,2,1,0:T(8,128)(2,1)} %pad_maximum_fusion.13), channel_id=1, source_target_pairs={{0,128},{8,136},{16,144},{24,152},{32,160},{40,168},{48,176},{56,1... | collective-permute-start | bytes 1966088 | tf_op jit(solution)/shard_map/ppermute | solution.py:18
  329.0 38.3 %collective-permute-start.42 = (bf16[2,5,256,128]{3,2,1,0:T(8,128)(2,1)}, bf16[2,5,256,128]{3,2,1,0:T(8,128)(2,1)}, u32[]{:S(2)}, u32[]{:S(2)}) collective-permute-start(bf16[2,5,256,128]{3,2,1,0:T(8,128)(2,1)} %pad_maximum_fusion.18), channel_id=1, source_target_pairs={{0,128},{8,136},{16,144},{24,152},{32,160},{40,168},{48,176},{56,1... | collective-permute-start | bytes 1966088 | tf_op jit(solution)/shard_map/ppermute | solution.py:18
  336.2 33.7 %collective-permute-start.19 = (bf16[2,5,256,128]{3,2,1,0:T(8,128)(2,1)}, bf16[2,5,256,128]{3,2,1,0:T(8,128)(2,1)}, u32[]{:S(2)}, u32[]{:S(2)}) collective-permute-start(bf16[2,5,256,128]{3,2,1,0:T(8,128)(2,1)} %pad_maximum_fusion.14), channel_id=1, source_target_pairs={{0,256},{8,264},{16,272},{24,280},{32,288},{40,296},{48,304},{56,3... | collective-permute-start | bytes 1966088 | tf_op jit(solution)/shard_map/ppermute | solution.py:18
  349.8 147.5 %collective-permute-start.53 = (bf16[2,5,256,128]{3,2,1,0:T(8,128)(2,1)}, bf16[2,5,256,128]{3,2,1,0:T(8,128)(2,1)}, u32[]{:S(2)}, u32[]{:S(2)}) collective-permute-start(bf16[2,5,256,128]{3,2,1,0:T(8,128)(2,1)} %pad_maximum_fusion.19), channel_id=1, source_target_pairs={{0,256},{8,264},{16,272},{24,280},{32,288},{40,296},{48,304},{56,3... | collective-permute-start | bytes 1966088 | tf_op jit(solution)/shard_map/ppermute | solution.py:18
  439.7 63.3 %collective-permute-start.54 = (f32[2,5,8]{2,1,0:T(8,128)}, f32[2,5,8]{2,1,0:T(8,128)}, u32[]{:S(2)}, u32[]{:S(2)}) collective-permute-start(f32[2,5,8]{2,1,0:T(8,128)} %pad_maximum_fusion.68), channel_id=1, source_target_pairs={{0,8},{8,0},{16,24},{24,16},{32,40},{40,32},{48,56},{56,48},{64,72... | collective-permute-start | bytes 968 | tf_op jit(solution)/shard_map/ppermute | solution.py:18
  482.1 182.9 %collective-permute-start.22 = (f32[2,5,128]{2,1,0:T(8,128)}, f32[2,5,128]{2,1,0:T(8,128)}, u32[]{:S(2)}, u32[]{:S(2)}) collective-permute-start(f32[2,5,128]{2,1,0:T(8,128)} %pad_maximum_fusion.60), channel_id=1, source_target_pairs={{0,8},{8,0},{16,24},{24,16},{32,40},{40,32},{48,56},{56,48},{64,72... | collective-permute-start | bytes 15368 | tf_op jit(solution)/shard_map/ppermute | solution.py:18
  484.6 151.5 %collective-permute-start.34 = (f32[2,5,32]{2,1,0:T(8,128)}, f32[2,5,32]{2,1,0:T(8,128)}, u32[]{:S(2)}, u32[]{:S(2)}) collective-permute-start(f32[2,5,32]{2,1,0:T(8,128)} %pad_maximum_fusion.61), channel_id=1, source_target_pairs={{0,8},{8,0},{16,24},{24,16},{32,40},{40,32},{48,56},{56,48},{64,72... | collective-permute-start | bytes 3848 | tf_op jit(solution)/shard_map/ppermute | solution.py:18
  489.3 156.0 %collective-permute-start.27 = (f32[2,5,64]{2,0,1:T(2,128)}, f32[2,5,64]{2,0,1:T(2,128)}, u32[]{:S(2)}, u32[]{:S(2)}) collective-permute-start(f32[2,5,64]{2,0,1:T(2,128)} %pad_maximum_fusion.73), channel_id=1, source_target_pairs={{0,8},{8,0},{16,24},{24,16},{32,40},{40,32},{48,56},{56,48},{64,72... | collective-permute-start | bytes 7688 | tf_op jit(solution)/shard_map/ppermute | solution.py:18
  497.3 188.9 %copy-start.58 = (bf16[2,5,256,128]{3,2,1,0:T(8,128)(2,1)S(1)}, bf16[2,5,256,128]{3,2,1,0:T(8,128)(2,1)}, u32[]{:S(2)}) copy-start(bf16[2,5,256,128]{3,2,1,0:T(8,128)(2,1)} %get-tuple-element.50) | copy-start | bytes 1966084
  497.3 188.9 %copy-start.60 = (bf16[2,5,256,128]{3,2,1,0:T(8,128)(2,1)S(1)}, bf16[2,5,256,128]{3,2,1,0:T(8,128)(2,1)}, u32[]{:S(2)}) copy-start(bf16[2,5,256,128]{3,2,1,0:T(8,128)(2,1)} %get-tuple-element.51) | copy-start | bytes 1966084
  497.3 188.9 %copy-start.121 = (pred[512,128]{1,0:T(8,128)(4,1)S(1)}, pred[512,128]{1,0:T(8,128)(4,1)}, u32[]{:S(2)}) copy-start(pred[512,128]{1,0:T(8,128)(4,1)} %fusion.138) | copy-start | bytes 196612
  497.3 128.1 %collective-permute-start.43 = (f32[2,5,16]{2,1,0:T(8,128)}, f32[2,5,16]{2,1,0:T(8,128)S(1)}, u32[]{:S(2)}, u32[]{:S(2)}) collective-permute-start(f32[2,5,16]{2,1,0:T(8,128)} %pad_maximum_fusion.64), channel_id=1, source_target_pairs={{0,8},{8,0},{16,24},{24,16},{32,40},{40,32},{48,56},{56,48},{64,72... | collective-permute-start | bytes 1928 | tf_op jit(solution)/shard_map/ppermute | solution.py:18
  503.8 123.6 %collective-permute-start.55 = (f32[2,5,16]{2,1,0:T(8,128)S(1)}, f32[2,5,16]{2,1,0:T(8,128)S(1)}, u32[]{:S(2)}, u32[]{:S(2)}) collective-permute-start(f32[2,5,16]{2,1,0:T(8,128)S(1)} %pad_maximum_fusion.69), channel_id=1, source_target_pairs={{0,16},{8,24},{16,0},{24,8},{32,48},{40,56},{48,32},{56,40},{64,80... | collective-permute-start | bytes 1928 | tf_op jit(solution)/shard_map/ppermute | solution.py:18
  625.5 14.8 %collective-permute-start.44 = (f32[2,5,32]{2,1,0:T(8,128)S(1)}, f32[2,5,32]{2,1,0:T(8,128)S(1)}, u32[]{:S(2)}, u32[]{:S(2)}) collective-permute-start(f32[2,5,32]{2,1,0:T(8,128)S(1)} %pad_maximum_fusion.65), channel_id=1, source_target_pairs={{0,16},{8,24},{16,0},{24,8},{32,48},{40,56},{48,32},{56,40},{64,80... | collective-permute-start | bytes 3848 | tf_op jit(solution)/shard_map/ppermute | solution.py:18
  627.6 14.8 %collective-permute-start.56 = (f32[2,5,32]{2,1,0:T(8,128)S(1)}, f32[2,5,32]{2,1,0:T(8,128)S(1)}, u32[]{:S(2)}, u32[]{:S(2)}) collective-permute-start(f32[2,5,32]{2,1,0:T(8,128)S(1)} %pad_maximum_fusion.70), channel_id=1, source_target_pairs={{0,32},{8,40},{16,48},{24,56},{32,0},{40,8},{48,16},{56,24},{64,96... | collective-permute-start | bytes 3848 | tf_op jit(solution)/shard_map/ppermute | solution.py:18
  636.9 12.6 %collective-permute-start.35 = (f32[2,5,64]{2,1,0:T(8,128)S(1)}, f32[2,5,64]{2,1,0:T(8,128)S(1)}, u32[]{:S(2)}, u32[]{:S(2)}) collective-permute-start(f32[2,5,64]{2,1,0:T(8,128)S(1)} %pad_maximum_fusion.62), channel_id=1, source_target_pairs={{0,16},{8,24},{16,0},{24,8},{32,48},{40,56},{48,32},{56,40},{64,80... | collective-permute-start | bytes 7688 | tf_op jit(solution)/shard_map/ppermute | solution.py:18
  640.4 11.2 %collective-permute-start.45 = (f32[2,5,64]{2,1,0:T(8,128)S(1)}, f32[2,5,64]{2,1,0:T(8,128)S(1)}, u32[]{:S(2)}, u32[]{:S(2)}) collective-permute-start(f32[2,5,64]{2,1,0:T(8,128)S(1)} %pad_maximum_fusion.66), channel_id=1, source_target_pairs={{0,32},{8,40},{16,48},{24,56},{32,0},{40,8},{48,16},{56,24},{64,96... | collective-permute-start | bytes 7688 | tf_op jit(solution)/shard_map/ppermute | solution.py:18
  642.5 16.5 %collective-permute-start.57 = (f32[2,5,64]{2,1,0:T(8,128)S(1)}, f32[2,5,64]{2,1,0:T(8,128)S(1)}, u32[]{:S(2)}, u32[]{:S(2)}) collective-permute-start(f32[2,5,64]{2,1,0:T(8,128)S(1)} %pad_maximum_fusion.71), channel_id=1, source_target_pairs={{0,64},{8,72},{16,80},{24,88},{32,96},{40,104},{48,112},{56,120},{... | collective-permute-start | bytes 7688 | tf_op jit(solution)/shard_map/ppermute | solution.py:18
  646.1 22.9 %collective-permute-start.28 = (f32[2,5,128]{2,0,1:T(2,128)S(1)}, f32[2,5,128]{2,0,1:T(2,128)S(1)}, u32[]{:S(2)}, u32[]{:S(2)}) collective-permute-start(f32[2,5,128]{2,0,1:T(2,128)S(1)} %pad_maximum_fusion.74), channel_id=1, source_target_pairs={{0,16},{8,24},{16,0},{24,8},{32,48},{40,56},{48,32},{56,40},{64,80... | collective-permute-start | bytes 15368 | tf_op jit(solution)/shard_map/ppermute | solution.py:18
  649.7 21.5 %collective-permute-start.36 = (f32[2,5,128]{2,1,0:T(8,128)S(1)}, f32[2,5,128]{2,1,0:T(8,128)S(1)}, u32[]{:S(2)}, u32[]{:S(2)}) collective-permute-start(f32[2,5,128]{2,1,0:T(8,128)S(1)} %pad_maximum_fusion.63), channel_id=1, source_target_pairs={{0,32},{8,40},{16,48},{24,56},{32,0},{40,8},{48,16},{56,24},{64,96... | collective-permute-start | bytes 15368 | tf_op jit(solution)/shard_map/ppermute | solution.py:18
  651.8 25.8 %collective-permute-start.46 = (f32[2,5,128]{2,1,0:T(8,128)S(1)}, f32[2,5,128]{2,1,0:T(8,128)S(1)}, u32[]{:S(2)}, u32[]{:S(2)}) collective-permute-start(f32[2,5,128]{2,1,0:T(8,128)S(1)} %pad_maximum_fusion.67), channel_id=1, source_target_pairs={{0,64},{8,72},{16,80},{24,88},{32,96},{40,104},{48,112},{56,120},{... | collective-permute-start | bytes 15368 | tf_op jit(solution)/shard_map/ppermute | solution.py:18
  659.2 23.2 %collective-permute-start.58 = (f32[2,5,128]{2,1,0:T(8,128)S(1)}, f32[2,5,128]{2,1,0:T(8,128)S(1)}, u32[]{:S(2)}, u32[]{:S(2)}) collective-permute-start(f32[2,5,128]{2,1,0:T(8,128)S(1)} %pad_maximum_fusion.72), channel_id=1, source_target_pairs={{0,128},{8,136},{16,144},{24,152},{32,160},{40,168},{48,176},{56,1... | collective-permute-start | bytes 15368 | tf_op jit(solution)/shard_map/ppermute | solution.py:18
  665.7 19.8 %collective-permute-start.23 = (f32[2,5,256]{2,1,0:T(8,128)S(1)}, f32[2,5,256]{2,1,0:T(8,128)S(1)}, u32[]{:S(2)}, u32[]{:S(2)}) collective-permute-start(f32[2,5,256]{2,1,0:T(8,128)S(1)} %pad_maximum_fusion.54), channel_id=1, source_target_pairs={{0,16},{8,24},{16,0},{24,8},{32,48},{40,56},{48,32},{56,40},{64,80... | collective-permute-start | bytes 30728 | tf_op jit(solution)/shard_map/ppermute | solution.py:18
  669.2 18.7 %collective-permute-start.29 = (f32[2,5,256]{2,0,1:T(2,128)S(1)}, f32[2,5,256]{2,0,1:T(2,128)S(1)}, u32[]{:S(2)}, u32[]{:S(2)}) collective-permute-start(f32[2,5,256]{2,0,1:T(2,128)S(1)} %pad_maximum_fusion.59), channel_id=1, source_target_pairs={{0,32},{8,40},{16,48},{24,56},{32,0},{40,8},{48,16},{56,24},{64,96... | collective-permute-start | bytes 30728 | tf_op jit(solution)/shard_map/ppermute | solution.py:18
  671.2 20.7 %collective-permute-start.37 = (f32[2,5,256]{2,1,0:T(8,128)S(1)}, f32[2,5,256]{2,1,0:T(8,128)}, u32[]{:S(2)}, u32[]{:S(2)}) collective-permute-start(f32[2,5,256]{2,1,0:T(8,128)S(1)} %pad_maximum_fusion.55), channel_id=1, source_target_pairs={{0,64},{8,72},{16,80},{24,88},{32,96},{40,104},{48,112},{56,120},{... | collective-permute-start | bytes 30728 | tf_op jit(solution)/shard_map/ppermute | solution.py:18
  677.7 18.5 %collective-permute-start.47 = (f32[2,5,256]{2,1,0:T(8,128)S(1)}, f32[2,5,256]{2,1,0:T(8,128)S(1)}, u32[]{:S(2)}, u32[]{:S(2)}) collective-permute-start(f32[2,5,256]{2,1,0:T(8,128)S(1)} %pad_maximum_fusion.56), channel_id=1, source_target_pairs={{0,128},{8,136},{16,144},{24,152},{32,160},{40,168},{48,176},{56,1... | collective-permute-start | bytes 30728 | tf_op jit(solution)/shard_map/ppermute | solution.py:18
  682.4 16.3 %collective-permute-start.59 = (f32[2,5,256]{2,1,0:T(8,128)S(1)}, f32[2,5,256]{2,1,0:T(8,128)S(1)}, u32[]{:S(2)}, u32[]{:S(2)}) collective-permute-start(f32[2,5,256]{2,1,0:T(8,128)S(1)} %pad_maximum_fusion.57), channel_id=1, source_target_pairs={{0,256},{8,264},{16,272},{24,280},{32,288},{40,296},{48,304},{56,3... | collective-permute-start | bytes 30728 | tf_op jit(solution)/shard_map/ppermute | solution.py:18
  (162 other events, 2394.2 us)
where the time goes:
time: 729 us; the launch traced here: 721 us
  starting transfers between devices  465 us (64%)
  local copies, waits for them, and re-layouts  97.8 us (13%)
  other arithmetic  72.7 us (10%)
  waiting for transfers between devices  47.5 us (7%)
  matrix products  34.6 us (5%)
    ppermute x60, starting transfers between devices, swapped(): return lax.ppermute(value, axis, pairs)  465 us
    ppermute x60, waiting for transfers between devices, swapped(): return lax.ppermute(value, axis, pairs)  47.5 us
    broadcast_in_dim x68, local copies, waits for them, and re-layouts, spread_rows(): widened = jnp.where(matches, source[:, :, None], filler)  36.7 us
    select_n x24, local copies, waits for them, and re-layouts, spread_rows(): widened = jnp.where(matches, source[:, :, None], filler)  26.4 us
    unnamed x347, local copies, waits for them, and re-layouts  16.2 us
    select_n x13, other arithmetic, double_up(): jnp.where(is_upper, stacked, partner)  15.5 us
  transfers between devices with their start and end apart: 60, of which 9 were waited for; matrix products, arithmetic and copies ran while one was open for 24% of the time, Pallas kernels for 0%

commit v1 on v0

v1 whole, which is shorter than its diff:
```python
import jax
import jax.numpy as jnp
from jax import lax
from jax.experimental import pallas as pl
from jax.experimental.pallas import tpu as pltpu
from jax.sharding import PartitionSpec as P

MESH = pl.DeviceIdType.MESH
F32 = jnp.float32
BF16 = jnp.bfloat16

SEQ_DEVICES = 64
HEADS = 5
LEVELS = 5
DH = 128
TOKENS = 128
SUB = 512
HALF = 256
SCALE = DH ** (-0.5)
MASKED = -1e30

GROUP = [4 << level for level in range(LEVELS)]
ROWS = [TOKENS >> level for level in range(LEVELS)]
PLACE = [
    [0, 1, 2, 3, 0],
    [2, 3, 4, 5, 1],
    [5, 6, 7, 9, 10],
    [3, 11, 14, 18, 27],
    [1, 13, 17, 45, 49],
]
SLOT = [[0, 0, 0, 0, 2], [1] * 5, [2] * 5, [2] * 5, [2] * 5]
FIRST = [0, 0, 64, 96, 112]
TILE_BASE = [0, 4, 12]


def dot(a, b, dims, precision=None):
    return lax.dot_general(a, b, (dims, ((), ())), precision=precision, preferred_element_type=F32)


def nn(a, b):
    return dot(a, b, ((1,), (0,)))


def nt(a, b):
    return dot(a, b, ((1,), (1,)))


def tn(a, b):
    return dot(a, b, ((0,), (0,)))


def position(index, off_ref, head):
    return jnp.where(
        index < 64,
        2 * index + off_ref[1, head],
        jnp.where(
            index < 96,
            4 * (index - 64) + off_ref[2, head],
            jnp.where(
                index < 112,
                8 * (index - 96) + off_ref[3, head],
                16 * ((index - 112) & 7) + off_ref[4, head],
            ),
        ),
    )


def kernel(
    q_ref, k_ref, v_ref, g_ref, off_ref,
    out_ref, lse_ref, dq_ref, dk_ref, dv_ref,
    s0, sbuf, s4, ubuf, u4, ebuf, dbuf, abuf, stbuf, stin, cout, cin, obuf, o4, r0, rbuf, r4,
    in_send, in_recv, st_send, st_recv, c_send, c_recv, res_send, res_recv,
):
    me = lax.axis_index("seq")
    inside = [lax.rem(me, g) for g in GROUP]
    start = [me - i for i in inside]

    level1 = jnp.int32(-1)
    head1 = jnp.int32(0)
    level2 = jnp.int32(-1)
    head2 = jnp.int32(0)
    for level in range(LEVELS):
        for head in range(HEADS):
            held = inside[level] == PLACE[level][head]
            if SLOT[level][head] == 1:
                level1 = jnp.where(held, level, level1)
                head1 = jnp.where(held, head, head1)
            elif SLOT[level][head] == 2:
                level2 = jnp.where(held, level, level2)
                head2 = jnp.where(held, head, head2)

    def level_of(u):
        return jnp.where(u == 0, 0, jnp.where(u == 1, level1, level2))

    def head_of(u):
        return jnp.where(u == 0, inside[0], jnp.where(u == 1, head1, head2))

    def tiles_of(u):
        return jnp.where(u == 0, TILE_BASE[0], jnp.where(u == 1, TILE_BASE[1], TILE_BASE[2]))

    def push(src, dst, target, send_sem, recv_sem):
        @pl.when(target != me)
        def _():
            pltpu.make_async_remote_copy(
                src_ref=src, dst_ref=dst, send_sem=send_sem, recv_sem=recv_sem,
                device_id={"seq": target}, device_id_type=MESH,
            ).start()

        @pl.when(target == me)
        def _():
            pltpu.make_async_copy(src, dst, recv_sem).start()

    def sent(src, target, send_sem):
        @pl.when(target != me)
        def _():
            pltpu.make_async_copy(src, src, send_sem).wait()

    def arrived(ref, sem):
        pltpu.make_async_copy(ref, ref, sem).wait()

    barrier = pltpu.get_barrier_semaphore()

    def greet(i, carry):
        pl.semaphore_signal(
            barrier, inc=1, device_id={"seq": lax.rem(me + 1 + i, SEQ_DEVICES)}, device_id_type=MESH
        )
        return carry

    lax.fori_loop(0, SEQ_DEVICES - 1, greet, 0)

    row = lax.broadcasted_iota(jnp.int32, (TOKENS, TOKENS), 0)
    col = lax.broadcasted_iota(jnp.int32, (TOKENS, TOKENS), 1)
    upper8 = lax.broadcasted_iota(jnp.int32, (16, 256), 0) < 8

    def select(head, carry):
        lanes = pl.ds(pl.multiple_of(head * DH, DH), DH)
        pair0 = jnp.concatenate([q_ref[:, lanes], k_ref[:, lanes]], axis=1)
        pair1 = jnp.concatenate([v_ref[:, lanes], g_ref[:, lanes]], axis=1)
        pick = (position(row, off_ref, head) == col).astype(F32).astype(BF16)
        sel0 = nn(pick, pair0)
        sel1 = nn(pick, pair1)
        s0[head, 0] = pair0
        s0[head, 1] = pair1
        sbuf[head, 0] = sel0[:112].astype(BF16)
        sbuf[head, 1] = sel1[:112].astype(BF16)
        s4[head] = jnp.where(upper8, sel0[112:], sel1[112:]).astype(BF16)
        return carry

    lax.fori_loop(0, HEADS, select, 0)

    pl.semaphore_wait(barrier, SEQ_DEVICES - 1)

    def in_copy(level, head):
        slot = SLOT[level][head]
        rows = ROWS[level]
        if level == 0:
            src = s0.at[head]
        elif level < 4:
            src = sbuf.at[head, :, pl.ds(FIRST[level], rows), :]
        else:
            src = s4.at[head]
        if level < 4:
            dst = ubuf.at[slot, :, pl.ds(pl.multiple_of(inside[level] * rows, rows), rows), :]
        else:
            dst = u4.at[me]
        return src, dst, start[level] + PLACE[level][head], in_send.at[level * HEADS + head], in_recv.at[slot]

    for level in range(LEVELS):
        for head in range(HEADS):
            push(*in_copy(level, head))

    key_i = lax.broadcasted_iota(jnp.int32, (HALF, HALF), 0)
    query_i = lax.broadcasted_iota(jnp.int32, (HALF, HALF), 1)
    causal = key_i <= query_i

    def forward(u, carry):
        level = level_of(u)
        head = head_of(u)

        @pl.when((level >= 0) & (level < 4))
        def _():
            arrived(ubuf.at[u], in_recv.at[u])

        @pl.when(level == 4)
        def _():
            arrived(u4, in_recv.at[u])

            def unpack(n, c):
                block = u4[pl.ds(n * 8, 8)].astype(F32)
                rows = pl.ds(pl.multiple_of(n * 64, 64), 64)
                ubuf[u, 0, rows, :] = block[:, :8, :].reshape(64, 256).astype(BF16)
                ubuf[u, 1, rows, :] = block[:, 8:, :].reshape(64, 256).astype(BF16)
                return c

            lax.fori_loop(0, 8, unpack, 0)

        @pl.when(level >= 0)
        def _():
            for j in range(2):
                keys = HALF * (j + 1)
                cols = pl.ds(j * HALF, HALF)
                q = ubuf[u, 0, cols, :DH]
                k = ubuf[u, 0, :keys, DH:]
                v = ubuf[u, 1, :keys, :DH]
                g = ubuf[u, 1, cols, DH:]
                s = nt(k, q) * SCALE
                last = jnp.where(causal, s[j * HALF :], MASKED)
                s = last if j == 0 else jnp.concatenate([s[:HALF], last], axis=0)
                m = jnp.max(s, axis=0, keepdims=True)
                e = jnp.exp(s - m)
                den = jnp.sum(e, axis=0, keepdims=True)
                ebuf[u, :keys, cols] = e
                abuf[u, :, cols] = tn(v, e.astype(BF16))
                dp = nt(v, g)
                dbuf[u, :keys, cols] = dp
                t = jnp.sum(e * dp, axis=0, keepdims=True)
                tile = jnp.concatenate([m, den, t, jnp.zeros((5, HALF), F32)], axis=0)
                stbuf[u, 2 * j] = tile[:, :128]
                stbuf[u, 2 * j + 1] = tile[:, 128:]

            first = me - lax.rem(me, 4 << level)

            def send_stats(i, c):
                push(
                    stbuf.at[u, lax.shift_right_logical(i, level)],
                    stin.at[level * HEADS + head],
                    first + i,
                    st_send.at[tiles_of(u) + i],
                    st_recv,
                )
                return c

            lax.fori_loop(0, 4 << level, send_stats, 0)

        return carry

    lax.fori_loop(0, 3, forward, 0)

    arrived(stin, st_recv)
    lane = lax.broadcasted_iota(jnp.int32, (1, TOKENS), 1)
    spread = [None]
    stats = [stin[:HEADS]]
    for level in range(1, LEVELS):
        base = (inside[level] & ((1 << level) - 1)) * ROWS[level]
        rep = (row == base + lax.shift_right_logical(col, level)).astype(F32)
        spread.append(rep)
        tiles = stin[level * HEADS : (level + 1) * HEADS].reshape(HEADS * 8, TOKENS)
        stats.append(dot(tiles, rep, ((1,), (0,)), lax.Precision.HIGHEST).reshape(HEADS, 8, TOKENS))
    answers = [[] for _ in range(LEVELS)]
    for head in range(HEADS):
        chosen = [None] + [
            (lane & ((1 << level) - 1)) == off_ref[level, head] for level in range(1, LEVELS)
        ]
        ms = [stats[0][head, 0:1]] + [
            jnp.where(chosen[level], stats[level][head, 0:1], MASKED) for level in range(1, LEVELS)
        ]
        top = ms[0]
        for level in range(1, LEVELS):
            top = jnp.maximum(top, ms[level])
        total = jnp.zeros((1, TOKENS), F32)
        delta = jnp.zeros((1, TOKENS), F32)
        for level in range(LEVELS):
            weight = jnp.exp(ms[level] - top)
            den, t = stats[level][head, 1:2], stats[level][head, 2:3]
            if level:
                den = jnp.where(chosen[level], den, 0.0)
                t = jnp.where(chosen[level], t, 0.0)
            total = total + den * weight
            delta = delta + t * weight
        log_total = top + jnp.log(total)
        delta = delta * jnp.exp(top - log_total)
        lse_ref[head : head + 1, :] = log_total
        answer = jnp.concatenate([log_total, delta, jnp.zeros((6, TOKENS), F32)], axis=0)
        for level in range(LEVELS):
            answers[level].append(answer if level == 0 else jnp.where(chosen[level], answer, 0.0))
    for level in range(LEVELS):
        if level:
            packed = dot(
                jnp.concatenate(answers[level], axis=0), spread[level], ((1,), (1,)), lax.Precision.HIGHEST
            ).reshape(HEADS, 8, TOKENS)
        for head in range(HEADS):
            cout[level * HEADS + head] = packed[head] if level else answers[0][head]

    def c_copy(level, head):
        slot = SLOT[level][head]
        n = level * HEADS + head
        return (
            cout.at[n], cin.at[TILE_BASE[slot] + inside[level]], start[level] + PLACE[level][head],
            c_send.at[n], c_recv.at[slot],
        )

    for level in range(LEVELS):
        for head in range(HEADS):
            push(*c_copy(level, head))

    def res_copy(u, level, i, head):
        rows = ROWS[level]
        if level < 4:
            src = obuf.at[u, :, pl.ds(pl.multiple_of(i * rows, rows), rows), :]
        else:
            src = o4.at[i]
        if level == 0:
            dst, sem = r0.at[head], res_recv.at[0]
        elif level < 4:
            dst, sem = rbuf.at[head, :, pl.ds(FIRST[level], rows), :], res_recv.at[1]
        else:
            dst, sem = r4.at[head], res_recv.at[2]
        return src, dst, start[level] + i, res_send.at[tiles_of(u) + i], sem

    def backward(u, carry):
        level = level_of(u)
        head = head_of(u)
        base = tiles_of(u)
        for lv in range(LEVELS):

            @pl.when(level == lv)
            def _():
                arrived(cin.at[pl.ds(base, GROUP[lv])], c_recv.at[u])

        @pl.when(level >= 0)
        def _():
            per = lax.shift_left(1, level)
            blocks = []
            for b in range(4):
                blocks.append(
                    lax.fori_loop(
                        0, per, lambda i, c: c + cin[base + b * per + i], jnp.zeros((8, TOKENS), F32)
                    )
                )
            dk = dv = None
            for j in range(2):
                keys = HALF * (j + 1)
                cols = pl.ds(j * HALF, HALF)
                q = ubuf[u, 0, cols, :DH]
                k = ubuf[u, 0, :keys, DH:]
                g = ubuf[u, 1, cols, DH:]
                answer = jnp.concatenate(blocks[2 * j : 2 * j + 2], axis=1)
                m = jnp.concatenate([stbuf[u, 2 * j], stbuf[u, 2 * j + 1]], axis=1)[0:1]
                w = jnp.exp(m - answer[0:1])
                delta = answer[1:2]
                p = ebuf[u, :keys, cols] * w
                ds = (SCALE * p * (dbuf[u, :keys, cols] - delta)).astype(BF16)
                p = p.astype(BF16)
                o = (abuf[u, :, cols] * w).T
                dq = tn(k, ds).T
                obuf[u, 0, cols, :DH] = o.astype(BF16)
                obuf[u, 0, cols, DH:] = dq.astype(BF16)
                dkj = nn(ds, q)
                dvj = nn(p, g)
                if j == 0:
                    dk, dv = dkj, dvj
                else:
                    obuf[u, 1, :HALF, :DH] = (dk + dkj[:HALF]).astype(BF16)
                    obuf[u, 1, :HALF, DH:] = (dv + dvj[:HALF]).astype(BF16)
                    obuf[u, 1, HALF:, :DH] = dkj[HALF:].astype(BF16)
                    obuf[u, 1, HALF:, DH:] = dvj[HALF:].astype(BF16)

        @pl.when(level == 4)
        def _():
            def pack(n, c):
                rows = pl.ds(pl.multiple_of(n * 64, 64), 64)
                lo = obuf[u, 0, rows, :].astype(F32).reshape(8, 8, 256)
                hi = obuf[u, 1, rows, :].astype(F32).reshape(8, 8, 256)
                o4[pl.ds(n * 8, 8)] = jnp.concatenate([lo, hi], axis=1).astype(BF16)
                return c

            lax.fori_loop(0, 8, pack, 0)

        for lv in range(LEVELS):

            @pl.when(level == lv)
            def _():
                def send_result(i, c):
                    push(*res_copy(u, lv, i, head))
                    return c

                lax.fori_loop(0, GROUP[lv], send_result, 0)

        return carry

    lax.fori_loop(0, 3, backward, 0)

    arrived(r0, res_recv.at[0])
    arrived(rbuf, res_recv.at[1])
    arrived(r4, res_recv.at[2])

    def finish(head, carry):
        lanes = pl.ds(pl.multiple_of(head * DH, DH), DH)
        hit = position(col, off_ref, head) == row
        put0 = (hit & (col < 120)).astype(F32).astype(BF16)
        put1 = (hit & ((col < 112) | (col >= 120))).astype(F32).astype(BF16)
        four = r4[head]
        all0 = r0[head, 0].astype(F32) + nn(put0, jnp.concatenate([rbuf[head, 0], four], axis=0))
        all1 = r0[head, 1].astype(F32) + nn(put1, jnp.concatenate([rbuf[head, 1], four], axis=0))
        out_ref[:, lanes] = all0[:, :DH].astype(BF16)
        dq_ref[:, lanes] = all0[:, DH:].astype(BF16)
        dk_ref[:, lanes] = all1[:, :DH].astype(BF16)
        dv_ref[:, lanes] = all1[:, DH:].astype(BF16)
        return carry

    lax.fori_loop(0, HEADS, finish, 0)

    for level in range(LEVELS):
        for head in range(HEADS):
            src, _, target, sem, _ = in_copy(level, head)
            sent(src, target, sem)
            src, _, target, sem, _ = c_copy(level, head)
            sent(src, target, sem)

    def drain(u, carry):
        level = level_of(u)
        for lv in range(LEVELS):

            @pl.when(level == lv)
            def _():
                def one(i, c):
                    src, _, target, sem, _ = res_copy(u, lv, i, 0)
                    sent(src, target, sem)
                    sent(stbuf.at[u, 0], target, st_send.at[tiles_of(u) + i])
                    return c

                lax.fori_loop(0, GROUP[lv], one, 0)

        return carry

    lax.fori_loop(0, 3, drain, 0)


def on_device(query_in, key_in, value_in, grad_out, offsets):
    flat = jax.ShapeDtypeStruct((TOKENS, HEADS * DH), BF16)
    vmem = pl.BlockSpec(memory_space=pltpu.VMEM)
    return pl.pallas_call(
        kernel,
        out_shape=(flat, jax.ShapeDtypeStruct((HEADS, TOKENS), F32), flat, flat, flat),
        in_specs=[vmem] * 4 + [pl.BlockSpec(memory_space=pltpu.SMEM)],
        out_specs=(vmem,) * 5,
        scratch_shapes=[
            pltpu.VMEM((HEADS, 2, TOKENS, 256), BF16),
            pltpu.VMEM((HEADS, 2, 112, 256), BF16),
            pltpu.VMEM((HEADS, 16, 256), BF16),
            pltpu.VMEM((3, 2, SUB, 256), BF16),
            pltpu.VMEM((SEQ_DEVICES, 16, 256), BF16),
            pltpu.VMEM((3, SUB, SUB), F32),
            pltpu.VMEM((3, SUB, SUB), F32),
            pltpu.VMEM((3, DH, SUB), F32),
            pltpu.VMEM((3, 4, 8, 128), F32),
            pltpu.VMEM((LEVELS * HEADS, 8, 128), F32),
            pltpu.VMEM((LEVELS * HEADS, 8, 128), F32),
            pltpu.VMEM((76, 8, 128), F32),
            pltpu.VMEM((3, 2, SUB, 256), BF16),
            pltpu.VMEM((SEQ_DEVICES, 16, 256), BF16),
            pltpu.VMEM((HEADS, 2, TOKENS, 256), BF16),
            pltpu.VMEM((HEADS, 2, 112, 256), BF16),
            pltpu.VMEM((HEADS, 16, 256), BF16),
            pltpu.SemaphoreType.DMA((LEVELS * HEADS,)),
            pltpu.SemaphoreType.DMA((3,)),
            pltpu.SemaphoreType.DMA((76,)),
            pltpu.SemaphoreType.DMA,
            pltpu.SemaphoreType.DMA((LEVELS * HEADS,)),
            pltpu.SemaphoreType.DMA((3,)),
            pltpu.SemaphoreType.DMA((76,)),
            pltpu.SemaphoreType.DMA((3,)),
        ],
        compiler_params=pltpu.CompilerParams(
            collective_id=0, has_side_effects=True, vmem_limit_bytes=48 * 1024 * 1024
        ),
    )(query_in, key_in, value_in, grad_out, offsets)


def solution(mesh):
    return jax.shard_map(
        on_device,
        mesh=mesh,
        in_specs=(P("seq", "head"),) * 4 + (P(None, "head"),),
        out_specs=(P("seq", "head"), P("head", "seq")) + (P("seq", "head"),) * 3,
        check_vma=False,
    )
```

time: 729 us -> 93.7 us (0.13)
  starting transfers between devices: 465 us -> 0 us
  local copies, waits for them, and re-layouts: 97.8 us -> 7.6 us
  Pallas kernels: 0 us -> 84.9 us
  other arithmetic: 72.7 us -> 0 us
  waiting for transfers between devices: 47.5 us -> 0 us
  matrix products: 34.6 us -> 0 us
    ppermute x60 -> x0, starting transfers between devices: 465 us -> none  [swapped(): return lax.ppermute(value, axis, pairs)]
    pallas_call x0 -> x1, Pallas kernels: none -> 84.9 us  [on_device(): pl.pallas_call(kernel, out_shape=(flat, jax.ShapeDtypeStruct((HEADS, TOKE...]
    ppermute x60 -> x0, waiting for transfers between devices: 47.5 us -> none  [swapped(): return lax.ppermute(value, axis, pairs)]
    broadcast_in_dim x68 -> x0, local copies, waits for them, and re-layouts: 36.7 us -> none  [spread_rows(): widened = jnp.where(matches, source[:, :, None], filler)]
    dot_general x30 -> x0, matrix products: 34.6 us -> none  [the longest x5 9.58 us: on_device(): jnp.einsum('hqk,hkd->hqd', score_grad, pair_group[0], preferred_element_t...]
    select_n x67 -> x0, other arithmetic: 32.2 us -> none  [the longest x13 15.5 us: double_up(): jnp.where(is_upper, stacked, partner)]
    select_n x24 -> x0, local copies, waits for them, and re-layouts: 26.4 us -> none  [spread_rows(): widened = jnp.where(matches, source[:, :, None], filler)]
    reduce_sum x16 -> x0, other arithmetic: 15.1 us -> none  [the longest x11 13.9 us: select_rows(): jnp.sum(jnp.where(matches, reshaped, zero), axis=2, dtype=source.dtype)]
  transfers between devices with their start and end apart: 60 -> 0, of which waited for: 9 -> 0; matrix products, arithmetic and copies ran while one was open for 24% -> 0% of each run, Pallas kernels for 0% -> 0%
where the time goes in v1:
time: 93.7 us; the launch traced here: 93.1 us
  Pallas kernels  84.9 us (91%)
  local copies, waits for them, and re-layouts  7.6 us (8%)
    pallas_call x1, Pallas kernels, on_device(): pl.pallas_call(kernel, out_shape=(flat, jax.ShapeDtypeStruct((HEADS, TOKE...  84.9 us
    unnamed x15, local copies, waits for them, and re-layouts  7.6 us

profile of v1, /device:TPU:1, one launch (start us, length us, event | category | flops | bytes accessed | tf_op | source)
XLA Modules:
  0.0 93.1 jit_solution(13485389659249712340)
XLA Ops:
  0.6 0.0 copy-start
  0.6 0.9 copy-done
  1.5 0.0 copy-start.1
  1.6 0.9 copy-done.1
  2.5 0.0 copy-start.2
  2.5 0.9 copy-done.2
  3.4 0.0 copy-start.3
  3.4 0.9 copy-done.3
  4.3 0.0 copy-start.4
  4.3 0.7 copy-done.4
  5.0 84.9 %shard_map.92 = (bf16[128,640]{1,0:T(8,128)(2,1)S(1)}, f32[5,128]{1,0:T(8,128)S(1)}, bf16[128,640]{1,0:T(8,128)(2,1)S(1)}, bf16[128,640]{1,0:T(8,128)(2,1)S(1)}, bf16[128,640]{1,0:T(8,128)(2,1)S(1)}) custom-call(bf16[128,640]{1,0:T(8,128)(2,1)S(1)} %copy-done, bf16[128,640]{1,0:T(8,128)(2,1)S(1)} %copy-done.1, bf16[128,640]{1,0:T(8,128)(2,1)S(1)} %copy-done.2, ...), custom_call_target="tpu_custom_call" | custom-call | tf_op jit(solution)/shard_map/pallas_call | solution.py:432
  89.9 0.7 copy.15
  90.5 0.6 copy.16
  91.1 0.7 copy.17
  91.8 0.7 copy.18
  92.5 0.7 copy.19
Async XLA Ops:
  0.6 0.9 copy-start
  1.5 0.9 copy-start.1
  2.5 0.9 copy-start.2
  3.4 0.9 copy-start.3
  4.3 0.7 copy-start.4

commit v2 on v1

v2 whole, which is shorter than its diff:
```python
import jax
import jax.numpy as jnp
from jax import lax
from jax.experimental import pallas as pl
from jax.experimental.pallas import tpu as pltpu
from jax.sharding import PartitionSpec as P

MESH = pl.DeviceIdType.MESH
F32 = jnp.float32
BF16 = jnp.bfloat16

SEQ_DEVICES = 64
HEADS = 5
LEVELS = 5
DH = 128
TOKENS = 128
SUB = 512
HALF = 256
SCALE = DH ** (-0.5)
MASKED = -1e30

GROUP = [2] + [4 << level for level in range(1, LEVELS)]
ROWS = [TOKENS >> level for level in range(LEVELS)]
PLACE = [
    None,
    [0, 2, 3, 4, 5],
    [0, 6, 7, 8, 9],
    [5, 15, 17, 28, 31],
    [1, 12, 33, 45, 52],
]
SLOTS = 5
FIRST = [0, 0, 64, 96, 112]
TILES = 2 * 3 + 8 + 64


def dot(a, b, dims, precision=None):
    return lax.dot_general(a, b, (dims, ((), ())), precision=precision, preferred_element_type=F32)


def nn(a, b):
    return dot(a, b, ((1,), (0,)))


def nt(a, b):
    return dot(a, b, ((1,), (1,)))


def tn(a, b):
    return dot(a, b, ((0,), (0,)))


def position(index, off_ref, head):
    return jnp.where(
        index < 64,
        2 * index + off_ref[1, head],
        jnp.where(
            index < 96,
            4 * (index - 64) + off_ref[2, head],
            jnp.where(
                index < 112,
                8 * (index - 96) + off_ref[3, head],
                16 * ((index - 112) & 7) + off_ref[4, head],
            ),
        ),
    )


def kernel(
    q_ref, k_ref, v_ref, g_ref, off_ref,
    out_ref, lse_ref, dq_ref, dk_ref, dv_ref,
    s0, sbuf, s4, ubuf, u4, ebuf, dbuf, abuf, stbuf, stin, cout, cin, acc, obuf, o4, r0, r0b, rbuf, r4,
    load_sem, in_send, kv_send, in_recv, kv_recv, st_send, st_recv, c_send, c_recv, res_send, res_kv_send, res_recv,
):
    me = lax.axis_index("seq")
    inside = [lax.rem(me, g) for g in GROUP]
    start = [me - i for i in inside]
    core = inside[0]
    upper = lax.rem(lax.div(me, 2), 2)

    level3 = jnp.int32(-1)
    head3 = jnp.int32(0)
    level4 = jnp.int32(-1)
    head4 = jnp.int32(0)
    for level in range(1, LEVELS):
        for head in range(HEADS):
            held = inside[level] == PLACE[level][head]
            if level == 1:
                level3 = jnp.where(held, level, level3)
                head3 = jnp.where(held, head, head3)
            else:
                level4 = jnp.where(held, level, level4)
                head4 = jnp.where(held, head, head4)

    def level_of(u):
        local = jnp.where((u == 2) & (core == 1), -1, 0)
        return jnp.where(u < 3, local, jnp.where(u == 3, level3, level4))

    def head_of(u):
        local = jnp.where(u == 2, 4, u + 2 * core)
        return jnp.where(u < 3, local, jnp.where(u == 3, head3, head4))

    def tiles_of(u):
        return jnp.where(u < 3, 2 * u, jnp.where(u == 3, 6, 14))

    def holder(level, head):
        if level == 0:
            return start[0] + (lax.div(head, 2) & 1), (head & 1) + 2 * lax.div(head, 4)
        place = jnp.int32(0)
        for h in range(HEADS):
            place = jnp.where(head == h, PLACE[level][h], place)
        return start[level] + place, 3 if level == 1 else 4

    def remote(src, dst, target, send_sem, recv_sem):
        pltpu.make_async_remote_copy(
            src_ref=src, dst_ref=dst, send_sem=send_sem, recv_sem=recv_sem,
            device_id={"seq": target}, device_id_type=MESH,
        ).start()

    def push(src, dst, target, send_sem, recv_sem):
        @pl.when(target != me)
        def _():
            remote(src, dst, target, send_sem, recv_sem)

        @pl.when(target == me)
        def _():
            pltpu.make_async_copy(src, dst, recv_sem).start()

    def done(src, send_sem):
        pltpu.make_async_copy(src, src, send_sem).wait()

    def sent(src, target, send_sem):
        @pl.when(target != me)
        def _():
            done(src, send_sem)

    arrived = done

    def load(head, carry):
        lanes = pl.ds(pl.multiple_of(head * DH, DH), DH)
        for pair, half, ref in ((0, 0, q_ref), (0, 1, g_ref), (1, 0, k_ref), (1, 1, v_ref)):
            pltpu.make_async_copy(
                ref.at[:, lanes], s0.at[head, pair, :, pl.ds(half * DH, DH)], load_sem
            ).start()
        return carry

    lax.fori_loop(0, HEADS, load, 0)

    barrier = pltpu.get_barrier_semaphore()

    def greet(i, carry):
        pl.semaphore_signal(
            barrier, inc=1, device_id={"seq": lax.rem(me + 1 + i, SEQ_DEVICES)}, device_id_type=MESH
        )
        return carry

    lax.fori_loop(0, SEQ_DEVICES - 1, greet, 0)

    row = lax.broadcasted_iota(jnp.int32, (TOKENS, TOKENS), 0)
    col = lax.broadcasted_iota(jnp.int32, (TOKENS, TOKENS), 1)
    upper8 = lax.broadcasted_iota(jnp.int32, (16, 256), 0) < 8
    arrived(s0, load_sem)

    def select(head, carry):
        pick = (position(row, off_ref, head) == col).astype(F32).astype(BF16)
        sel0 = nn(pick, s0[head, 0])
        sel1 = nn(pick, s0[head, 1])
        sbuf[head, 0] = sel0[:112].astype(BF16)
        sbuf[head, 1] = sel1[:112].astype(BF16)
        s4[head] = jnp.where(upper8, sel0[112:], sel1[112:]).astype(BF16)
        return carry

    lax.fori_loop(0, HEADS, select, 0)

    pl.semaphore_wait(barrier, SEQ_DEVICES - 1)

    def in_copy(level, head):
        rows = ROWS[level]
        target, slot = holder(level, head)
        if level == 0:
            src = s0.at[head]
            at = upper * HALF + core * TOKENS
        elif level < 4:
            src = sbuf.at[head, :, pl.ds(FIRST[level], rows), :]
            at = inside[level] * rows
        else:
            src = s4.at[head]
        if level < 4:
            dst = ubuf.at[slot, :, pl.ds(pl.multiple_of(at, rows), rows), :]
        else:
            dst = u4.at[me]
        return src, dst, target, in_send.at[level * HEADS + head], in_recv.at[slot]

    def kv_copy(head):
        target, slot = holder(0, head)
        at = pl.ds(pl.multiple_of(core * TOKENS, TOKENS), TOKENS)
        return s0.at[head, 1], ubuf.at[slot, 1, at, :], target + 2, kv_send.at[head], kv_recv.at[slot]

    turn = lax.div(me, 2)
    for level in range(LEVELS - 1, -1, -1):

        def send_rows(i, carry):
            head = lax.rem(turn + i, HEADS)
            push(*in_copy(level, head))
            if level == 0:

                @pl.when(upper == 0)
                def _():
                    remote(*kv_copy(head))

            return carry

        lax.fori_loop(0, HEADS, send_rows, 0)

    key_i = lax.broadcasted_iota(jnp.int32, (HALF, HALF), 0)
    query_i = lax.broadcasted_iota(jnp.int32, (HALF, HALF), 1)
    causal = key_i <= query_i

    def does(level, j):
        return (level > 0) | ((level == 0) & (upper == j))

    def forward(step, carry):
        u = SLOTS - 1 - step
        level = level_of(u)
        head = head_of(u)

        @pl.when(level == 0)
        def _():
            arrived(ubuf.at[u, :, pl.ds(0, HALF), :], in_recv.at[u])

            @pl.when(upper == 1)
            def _():
                arrived(ubuf.at[u, 1, pl.ds(0, HALF), :], kv_recv.at[u])

        @pl.when((level > 0) & (level < 4))
        def _():
            arrived(ubuf.at[u], in_recv.at[u])

        @pl.when(level == 4)
        def _():
            arrived(u4, in_recv.at[u])

            def unpack(n, c):
                block = u4[pl.ds(n * 8, 8)].astype(F32)
                rows = pl.ds(pl.multiple_of(n * 64, 64), 64)
                ubuf[u, 0, rows, :] = block[:, :8, :].reshape(64, 256).astype(BF16)
                ubuf[u, 1, rows, :] = block[:, 8:, :].reshape(64, 256).astype(BF16)
                return c

            lax.fori_loop(0, 8, unpack, 0)

        for j in range(2):

            @pl.when(does(level, j))
            def _():
                keys = HALF * (j + 1)
                cols = pl.ds(j * HALF, HALF)
                q = ubuf[u, 0, cols, :DH]
                g = ubuf[u, 0, cols, DH:]
                k = ubuf[u, 1, :keys, :DH]
                v = ubuf[u, 1, :keys, DH:]
                s = nt(k, q) * SCALE
                last = jnp.where(causal, s[j * HALF :], MASKED)
                s = last if j == 0 else jnp.concatenate([s[:HALF], last], axis=0)
                m = jnp.max(s, axis=0, keepdims=True)
                e = jnp.exp(s - m)
                den = jnp.sum(e, axis=0, keepdims=True)
                ebuf[u, :keys, cols] = e
                abuf[u, :, cols] = tn(v, e.astype(BF16))
                dp = nt(v, g)
                dbuf[u, :keys, cols] = dp
                t = jnp.sum(e * dp, axis=0, keepdims=True)
                tile = jnp.concatenate([m, den, t, jnp.zeros((5, HALF), F32)], axis=0)
                stbuf[u, 2 * j] = tile[:, :128]
                stbuf[u, 2 * j + 1] = tile[:, 128:]

        @pl.when(level >= 0)
        def _():
            count = jnp.where(level == 0, 2, 4 << level)
            first = me - lax.rem(me, count)
            block = jnp.where(level == 0, 2 * upper, 0)

            def send_stats(i, c):
                push(
                    stbuf.at[u, block + lax.shift_right_logical(i, level)],
                    stin.at[level * HEADS + head],
                    first + i,
                    st_send.at[tiles_of(u) + i],
                    st_recv,
                )
                return c

            lax.fori_loop(0, count, send_stats, 0)

        return carry

    lax.fori_loop(0, SLOTS, forward, 0)

    arrived(stin, st_recv)
    lane = lax.broadcasted_iota(jnp.int32, (1, TOKENS), 1)
    spread = [None]
    stats = [stin[:HEADS]]
    for level in range(1, LEVELS):
        base = (inside[level] & ((1 << level) - 1)) * ROWS[level]
        rep = (row == base + lax.shift_right_logical(col, level)).astype(F32)
        spread.append(rep)
        tiles = stin[level * HEADS : (level + 1) * HEADS].reshape(HEADS * 8, TOKENS)
        stats.append(dot(tiles, rep, ((1,), (0,)), lax.Precision.HIGHEST).reshape(HEADS, 8, TOKENS))
    answers = [[] for _ in range(LEVELS)]
    for head in range(HEADS):
        chosen = [None] + [
            (lane & ((1 << level) - 1)) == off_ref[level, head] for level in range(1, LEVELS)
        ]
        ms = [stats[0][head, 0:1]] + [
            jnp.where(chosen[level], stats[level][head, 0:1], MASKED) for level in range(1, LEVELS)
        ]
        top = ms[0]
        for level in range(1, LEVELS):
            top = jnp.maximum(top, ms[level])
        total = jnp.zeros((1, TOKENS), F32)
        delta = jnp.zeros((1, TOKENS), F32)
        for level in range(LEVELS):
            weight = jnp.exp(ms[level] - top)
            den, t = stats[level][head, 1:2], stats[level][head, 2:3]
            if level:
                den = jnp.where(chosen[level], den, 0.0)
                t = jnp.where(chosen[level], t, 0.0)
            total = total + den * weight
            delta = delta + t * weight
        log_total = top + jnp.log(total)
        delta = delta * jnp.exp(top - log_total)
        lse_ref[head : head + 1, :] = log_total
        answer = jnp.concatenate([log_total, delta, jnp.zeros((6, TOKENS), F32)], axis=0)
        for level in range(LEVELS):
            answers[level].append(answer if level == 0 else jnp.where(chosen[level], answer, 0.0))

    def c_copy(level, head):
        n = level * HEADS + head
        target, slot = holder(level, head)
        return cout.at[n], cin.at[tiles_of(slot) + inside[level]], target, c_send.at[n], c_recv.at[slot]

    for level in range(LEVELS - 1, -1, -1):
        if level:
            packed = dot(
                jnp.concatenate(answers[level], axis=0), spread[level], ((1,), (1,)), lax.Precision.HIGHEST
            ).reshape(HEADS, 8, TOKENS)
        for head in range(HEADS):
            cout[level * HEADS + head] = packed[head] if level else answers[0][head]

        def send_answer(i, carry):
            push(*c_copy(level, lax.rem(turn + i, HEADS)))
            return carry

        lax.fori_loop(0, HEADS, send_answer, 0)

    def res_copy(u, level, i, head):
        rows = ROWS[level]
        if level < 4:
            at = i * rows if level else upper * HALF + i * rows
            src = obuf.at[u, :, pl.ds(pl.multiple_of(at, rows), rows), :]
        else:
            src = o4.at[i]
        if level == 0:
            dst, sem = r0.at[head], res_recv.at[0]
        elif level < 4:
            dst, sem = rbuf.at[head, :, pl.ds(FIRST[level], rows), :], res_recv.at[1]
        else:
            dst, sem = r4.at[head], res_recv.at[2]
        return src, dst, start[level] + i, res_send.at[tiles_of(u) + i], sem

    def res_kv_copy(u, i, head):
        src = obuf.at[u, 1, pl.ds(pl.multiple_of(i * TOKENS, TOKENS), TOKENS), :]
        return src, r0b.at[head], start[0] - 2 + i, res_kv_send.at[2 * u + i], res_recv.at[3]

    def backward(step, carry):
        u = SLOTS - 1 - step
        level = level_of(u)
        head = head_of(u)
        base = tiles_of(u)
        for lv in range(LEVELS):

            @pl.when(level == lv)
            def _():
                arrived(cin.at[pl.ds(base, GROUP[lv])], c_recv.at[u])

        per = lax.shift_left(1, jnp.maximum(level, 0))
        origin = jnp.where(level == 0, base - 2 * upper, base)

        for j in range(2):

            @pl.when(does(level, j))
            def _():
                blocks = []
                for b in range(2 * j, 2 * j + 2):
                    blocks.append(
                        lax.fori_loop(
                            0, per, lambda i, c: c + cin[origin + b * per + i], jnp.zeros((8, TOKENS), F32)
                        )
                    )
                keys = HALF * (j + 1)
                cols = pl.ds(j * HALF, HALF)
                q = ubuf[u, 0, cols, :DH]
                g = ubuf[u, 0, cols, DH:]
                k = ubuf[u, 1, :keys, :DH]
                answer = jnp.concatenate(blocks, axis=1)
                m = jnp.concatenate([stbuf[u, 2 * j], stbuf[u, 2 * j + 1]], axis=1)[0:1]
                w = jnp.exp(m - answer[0:1])
                delta = answer[1:2]
                p = ebuf[u, :keys, cols] * w
                ds = (SCALE * p * (dbuf[u, :keys, cols] - delta)).astype(BF16)
                p = p.astype(BF16)
                o = (abuf[u, :, cols] * w).T
                dq = tn(k, ds).T
                obuf[u, 0, cols, :DH] = o.astype(BF16)
                obuf[u, 0, cols, DH:] = dq.astype(BF16)
                dk = nn(ds, q)
                dv = nn(p, g)
                if j == 0:
                    acc[:, :DH] = dk
                    acc[:, DH:] = dv
                    obuf[u, 1, :HALF, :DH] = dk.astype(BF16)
                    obuf[u, 1, :HALF, DH:] = dv.astype(BF16)
                else:
                    both = level > 0
                    obuf[u, 1, :HALF, :DH] = (dk[:HALF] + jnp.where(both, acc[:, :DH], 0.0)).astype(BF16)
                    obuf[u, 1, :HALF, DH:] = (dv[:HALF] + jnp.where(both, acc[:, DH:], 0.0)).astype(BF16)
                    obuf[u, 1, HALF:, :DH] = dk[HALF:].astype(BF16)
                    obuf[u, 1, HALF:, DH:] = dv[HALF:].astype(BF16)

        @pl.when(level == 4)
        def _():
            def pack(n, c):
                rows = pl.ds(pl.multiple_of(n * 64, 64), 64)
                lo = obuf[u, 0, rows, :].astype(F32).reshape(8, 8, 256)
                hi = obuf[u, 1, rows, :].astype(F32).reshape(8, 8, 256)
                o4[pl.ds(n * 8, 8)] = jnp.concatenate([lo, hi], axis=1).astype(BF16)
                return c

            lax.fori_loop(0, 8, pack, 0)

        for lv in range(LEVELS):

            @pl.when(level == lv)
            def _():
                def send_result(i, c):
                    push(*res_copy(u, lv, lax.rem(i + turn, GROUP[lv]), head))
                    if lv == 0:

                        @pl.when(upper == 1)
                        def _():
                            remote(*res_kv_copy(u, i, head))

                    return c

                lax.fori_loop(0, GROUP[lv], send_result, 0)

        return carry

    lax.fori_loop(0, SLOTS, backward, 0)

    arrived(r4, res_recv.at[2])
    arrived(rbuf, res_recv.at[1])
    arrived(r0, res_recv.at[0])

    @pl.when(upper == 0)
    def _():
        arrived(r0b, res_recv.at[3])

    def finish(head, carry):
        lanes = pl.ds(pl.multiple_of(head * DH, DH), DH)
        hit = position(col, off_ref, head) == row
        put0 = (hit & (col < 120)).astype(F32).astype(BF16)
        put1 = (hit & ((col < 112) | (col >= 120))).astype(F32).astype(BF16)
        four = r4[head]
        all0 = r0[head, 0].astype(F32) + nn(put0, jnp.concatenate([rbuf[head, 0], four], axis=0))
        all1 = r0[head, 1].astype(F32) + nn(put1, jnp.concatenate([rbuf[head, 1], four], axis=0))
        all1 = all1 + jnp.where(upper == 0, r0b[head].astype(F32), 0.0)
        out_ref[:, lanes] = all0[:, :DH].astype(BF16)
        dq_ref[:, lanes] = all0[:, DH:].astype(BF16)
        dk_ref[:, lanes] = all1[:, :DH].astype(BF16)
        dv_ref[:, lanes] = all1[:, DH:].astype(BF16)
        return carry

    lax.fori_loop(0, HEADS, finish, 0)

    def drain_own(head, carry):
        for level in range(LEVELS):
            src, _, target, sem, _ = in_copy(level, head)
            sent(src, target, sem)
            src, _, target, sem, _ = c_copy(level, head)
            sent(src, target, sem)

        @pl.when(upper == 0)
        def _():
            src, _, _, sem, _ = kv_copy(head)
            done(src, sem)

        return carry

    lax.fori_loop(0, HEADS, drain_own, 0)

    def drain(u, carry):
        level = level_of(u)
        for lv in range(LEVELS):

            @pl.when(level == lv)
            def _():
                def one(i, c):
                    src, _, target, sem, _ = res_copy(u, lv, i, 0)
                    sent(src, target, sem)
                    sent(stbuf.at[u, 0], target, st_send.at[tiles_of(u) + i])
                    if lv == 0:

                        @pl.when(upper == 1)
                        def _():
                            src, _, _, sem, _ = res_kv_copy(u, i, 0)
                            done(src, sem)

                    return c

                lax.fori_loop(0, GROUP[lv], one, 0)

        return carry

    lax.fori_loop(0, SLOTS, drain, 0)


def on_device(query_in, key_in, value_in, grad_out, offsets):
    flat = jax.ShapeDtypeStruct((TOKENS, HEADS * DH), BF16)
    vmem = pl.BlockSpec(memory_space=pltpu.VMEM)
    return pl.pallas_call(
        kernel,
        out_shape=(flat, jax.ShapeDtypeStruct((HEADS, TOKENS), F32), flat, flat, flat),
        in_specs=[pl.BlockSpec(memory_space=pl.ANY)] * 4 + [pl.BlockSpec(memory_space=pltpu.SMEM)],
        out_specs=(vmem,) * 5,
        scratch_shapes=[
            pltpu.VMEM((HEADS, 2, TOKENS, 256), BF16),
            pltpu.VMEM((HEADS, 2, 112, 256), BF16),
            pltpu.VMEM((HEADS, 16, 256), BF16),
            pltpu.VMEM((SLOTS, 2, SUB, 256), BF16),
            pltpu.VMEM((SEQ_DEVICES, 16, 256), BF16),
            pltpu.VMEM((SLOTS, SUB, SUB), F32),
            pltpu.VMEM((SLOTS, SUB, SUB), F32),
            pltpu.VMEM((SLOTS, DH, SUB), F32),
            pltpu.VMEM((SLOTS, 4, 8, 128), F32),
            pltpu.VMEM((LEVELS * HEADS, 8, 128), F32),
            pltpu.VMEM((LEVELS * HEADS, 8, 128), F32),
            pltpu.VMEM((TILES, 8, 128), F32),
            pltpu.VMEM((HALF, 256), F32),
            pltpu.VMEM((SLOTS, 2, SUB, 256), BF16),
            pltpu.VMEM((SEQ_DEVICES, 16, 256), BF16),
            pltpu.VMEM((HEADS, 2, TOKENS, 256), BF16),
            pltpu.VMEM((HEADS, TOKENS, 256), BF16),
            pltpu.VMEM((HEADS, 2, 112, 256), BF16),
            pltpu.VMEM((HEADS, 16, 256), BF16),
            pltpu.SemaphoreType.DMA,
            pltpu.SemaphoreType.DMA((LEVELS * HEADS,)),
            pltpu.SemaphoreType.DMA((HEADS,)),
            pltpu.SemaphoreType.DMA((SLOTS,)),
            pltpu.SemaphoreType.DMA((3,)),
            pltpu.SemaphoreType.DMA((TILES,)),
            pltpu.SemaphoreType.DMA,
            pltpu.SemaphoreType.DMA((LEVELS * HEADS,)),
            pltpu.SemaphoreType.DMA((SLOTS,)),
            pltpu.SemaphoreType.DMA((TILES,)),
            pltpu.SemaphoreType.DMA((6,)),
            pltpu.SemaphoreType.DMA((4,)),
        ],
        compiler_params=pltpu.CompilerParams(
            collective_id=0, has_side_effects=True, vmem_limit_bytes=60 * 1024 * 1024
        ),
    )(query_in, key_in, value_in, grad_out, offsets)


def solution(mesh):
    return jax.shard_map(
        on_device,
        mesh=mesh,
        in_specs=(P("seq", "head"),) * 4 + (P(None, "head"),),
        out_specs=(P("seq", "head"), P("head", "seq")) + (P("seq", "head"),) * 3,
        check_vma=False,
    )
```

time: 93.7 us -> 83.2 us (0.89)
  the two profiles are of different devices: /device:TPU:1 before, /device:TPU:31 now
where the time goes in v2:
time: 83.2 us; the launch traced here: 82.9 us
  Pallas kernels  77.4 us (93%)
  local copies, waits for them, and re-layouts  4.85 us (6%)
    pallas_call x1, Pallas kernels, on_device(): pl.pallas_call(kernel, out_shape=(flat, jax.ShapeDtypeStruct((HEADS, TOKE...  77.4 us
    unnamed x13, local copies, waits for them, and re-layouts  4.85 us

profile of v2, /device:TPU:31, one launch (start us, length us, event | category | flops | bytes accessed | tf_op | source)
XLA Modules:
  0.0 82.9 jit_solution(18136828838499754321)
XLA Ops:
  0.6 77.4 %shard_map.92 = (bf16[128,640]{1,0:T(8,128)(2,1)}, f32[5,128]{1,0:T(8,128)}, bf16[128,640]{1,0:T(8,128)(2,1)}, bf16[128,640]{1,0:T(8,128)(2,1)}, bf16[128,640]{1,0:T(8,128)(2,1)}) custom-call(bf16[128,640]{1,0:T(8,128)(2,1)} %q_ref.1, bf16[128,640]{1,0:T(8,128)(2,1)} %k_ref.1, bf16[128,640]{1,0:T(8,128)(2,1)} %v_ref.1, bf16[128,640]{1,0:T(8,128)(2,1)} %g_ref.1, ...), custom_call_target="tpu_custom_call" | custom-call | tf_op jit(solution)/shard_map/pallas_call | solution.py:530
  78.1 0.0 copy-start.3
  78.1 0.0 copy-start.2
  78.1 1.6 %copy.15 = bf16[128,640]{1,0:T(8,128)(2,1)} copy(bf16[128,640]{1,0:T(8,128)(2,1)} %get-tuple-element.10) | data formatting | bytes 327680
  79.7 0.0 copy-done.3
  79.7 0.6 copy.16
  80.3 0.0 copy-done.2
  80.3 0.0 copy-start.1
  80.3 0.7 copy.17
  81.0 0.3 copy-done.1
  81.3 0.0 copy-start
  81.3 0.7 copy.18
  82.0 0.3 copy-done
  82.3 0.7 copy.19
Async XLA Ops:
  78.1 1.7 %copy-start.3 = (f32[5,128]{1,0:T(8,128)S(1)}, f32[5,128]{1,0:T(8,128)}, u32[]{:S(2)}) copy-start(f32[5,128]{1,0:T(8,128)} %get-tuple-element.11) | copy-start | bytes 7684
  78.1 2.2 %copy-start.2 = (bf16[128,640]{1,0:T(8,128)(2,1)S(1)}, bf16[128,640]{1,0:T(8,128)(2,1)}, u32[]{:S(2)}) copy-start(bf16[128,640]{1,0:T(8,128)(2,1)} %get-tuple-element.12) | copy-start | bytes 491524
  80.3 1.0 %copy-start.1 = (bf16[128,640]{1,0:T(8,128)(2,1)S(1)}, bf16[128,640]{1,0:T(8,128)(2,1)}, u32[]{:S(2)}) copy-start(bf16[128,640]{1,0:T(8,128)(2,1)} %get-tuple-element.13) | copy-start | bytes 491524
  81.3 1.0 %copy-start = (bf16[128,640]{1,0:T(8,128)(2,1)S(1)}, bf16[128,640]{1,0:T(8,128)(2,1)}, u32[]{:S(2)}) copy-start(bf16[128,640]{1,0:T(8,128)(2,1)} %get-tuple-element.14) | copy-start | bytes 491524

commit v3 on v2

--- a/solution.py
+++ b/solution.py
@@ -33,8 +33,8 @@
 TILES = 2 * 3 + 8 + 64
 
 
-def dot(a, b, dims, precision=None):
-    return lax.dot_general(a, b, (dims, ((), ())), precision=precision, preferred_element_type=F32)
+def dot(a, b, dims):
+    return lax.dot_general(a, b, (dims, ((), ())), preferred_element_type=F32)
 
 
 def nn(a, b):
@@ -47,6 +47,15 @@
 
 def tn(a, b):
     return dot(a, b, ((0,), (0,)))
+
+
+def move(tiles, rep, dims):
+    rows = tiles.shape[0]
+    high = tiles.astype(BF16).astype(F32)
+    mid = (tiles - high).astype(BF16).astype(F32)
+    low = tiles - high - mid
+    out = dot(jnp.concatenate([high, mid, low], axis=0).astype(BF16), rep, dims)
+    return (out[2 * rows :] + out[rows : 2 * rows]) + out[:rows]
 
 
 def position(index, off_ref, head):
@@ -67,8 +76,8 @@
 
 def kernel(
     q_ref, k_ref, v_ref, g_ref, off_ref,
-    out_ref, lse_ref, dq_ref, dk_ref, dv_ref,
-    s0, sbuf, s4, ubuf, u4, ebuf, dbuf, abuf, stbuf, stin, cout, cin, acc, obuf, o4, r0, r0b, rbuf, r4,
+    lse_ref, r0, r0b, rbuf, r4,
+    s0, sbuf, s4, ubuf, u4, ebuf, dbuf, abuf, stbuf, stin, cout, cin, acc, obuf, o4,
     load_sem, in_send, kv_send, in_recv, kv_recv, st_send, st_recv, c_send, c_recv, res_send, res_kv_send, res_recv,
 ):
     me = lax.axis_index("seq")
@@ -135,6 +144,16 @@
 
     arrived = done
 
+    barrier = pltpu.get_barrier_semaphore()
+
+    def greet(i, carry):
+        pl.semaphore_signal(
+            barrier, inc=1, device_id={"seq": lax.rem(me + 1 + lax.rem(i + 15, 63), SEQ_DEVICES)}, device_id_type=MESH
+        )
+        return carry
+
+    lax.fori_loop(0, SEQ_DEVICES - 1, greet, 0)
+
     def load(head, carry):
         lanes = pl.ds(pl.multiple_of(head * DH, DH), DH)
         for pair, half, ref in ((0, 0, q_ref), (0, 1, g_ref), (1, 0, k_ref), (1, 1, v_ref)):
@@ -144,16 +163,6 @@
         return carry
 
     lax.fori_loop(0, HEADS, load, 0)
-
-    barrier = pltpu.get_barrier_semaphore()
-
-    def greet(i, carry):
-        pl.semaphore_signal(
-            barrier, inc=1, device_id={"seq": lax.rem(me + 1 + i, SEQ_DEVICES)}, device_id_type=MESH
-        )
-        return carry
-
-    lax.fori_loop(0, SEQ_DEVICES - 1, greet, 0)
 
     row = lax.broadcasted_iota(jnp.int32, (TOKENS, TOKENS), 0)
     col = lax.broadcasted_iota(jnp.int32, (TOKENS, TOKENS), 1)
@@ -301,10 +310,10 @@
     stats = [stin[:HEADS]]
     for level in range(1, LEVELS):
         base = (inside[level] & ((1 << level) - 1)) * ROWS[level]
-        rep = (row == base + lax.shift_right_logical(col, level)).astype(F32)
+        rep = (row == base + lax.shift_right_logical(col, level)).astype(F32).astype(BF16)
         spread.append(rep)
         tiles = stin[level * HEADS : (level + 1) * HEADS].reshape(HEADS * 8, TOKENS)
-        stats.append(dot(tiles, rep, ((1,), (0,)), lax.Precision.HIGHEST).reshape(HEADS, 8, TOKENS))
+        stats.append(move(tiles, rep, ((1,), (0,))).reshape(HEADS, 8, TOKENS))
     answers = [[] for _ in range(LEVELS)]
     for head in range(HEADS):
         chosen = [None] + [
@@ -340,9 +349,8 @@
 
     for level in range(LEVELS - 1, -1, -1):
         if level:
-            packed = dot(
-                jnp.concatenate(answers[level], axis=0), spread[level], ((1,), (1,)), lax.Precision.HIGHEST
-            ).reshape(HEADS, 8, TOKENS)
+            packed = move(jnp.concatenate(answers[level], axis=0), spread[level], ((1,), (1,)))
+            packed = packed.reshape(HEADS, 8, TOKENS)
         for head in range(HEADS):
             cout[level * HEADS + head] = packed[head] if level else answers[0][head]
 
@@ -371,8 +379,7 @@
         src = obuf.at[u, 1, pl.ds(pl.multiple_of(i * TOKENS, TOKENS), TOKENS), :]
         return src, r0b.at[head], start[0] - 2 + i, res_kv_send.at[2 * u + i], res_recv.at[3]
 
-    def backward(step, carry):
-        u = SLOTS - 1 - step
+    def backward(u, carry):
         level = level_of(u)
         head = head_of(u)
         base = tiles_of(u)
@@ -465,23 +472,6 @@
     def _():
         arrived(r0b, res_recv.at[3])
 
-    def finish(head, carry):
-        lanes = pl.ds(pl.multiple_of(head * DH, DH), DH)
-        hit = position(col, off_ref, head) == row
-        put0 = (hit & (col < 120)).astype(F32).astype(BF16)
-        put1 = (hit & ((col < 112) | (col >= 120))).astype(F32).astype(BF16)
-        four = r4[head]
-        all0 = r0[head, 0].astype(F32) + nn(put0, jnp.concatenate([rbuf[head, 0], four], axis=0))
-        all1 = r0[head, 1].astype(F32) + nn(put1, jnp.concatenate([rbuf[head, 1], four], axis=0))
-        all1 = all1 + jnp.where(upper == 0, r0b[head].astype(F32), 0.0)
-        out_ref[:, lanes] = all0[:, :DH].astype(BF16)
-        dq_ref[:, lanes] = all0[:, DH:].astype(BF16)
-        dk_ref[:, lanes] = all1[:, :DH].astype(BF16)
-        dv_ref[:, lanes] = all1[:, DH:].astype(BF16)
-        return carry
-
-    lax.fori_loop(0, HEADS, finish, 0)
-
     def drain_own(head, carry):
         for level in range(LEVELS):
             src, _, target, sem, _ = in_copy(level, head)
@@ -524,14 +514,39 @@
     lax.fori_loop(0, SLOTS, drain, 0)
 
 
+def finish(off_ref, lse_ref, r0, r0b, rbuf, r4, out_ref, log_ref, dq_ref, dk_ref, dv_ref):
+    head = pl.program_id(0)
+    upper = lax.rem(lax.div(lax.axis_index("seq"), 2), 2)
+    row = lax.broadcasted_iota(jnp.int32, (TOKENS, TOKENS), 0)
+    col = lax.broadcasted_iota(jnp.int32, (TOKENS, TOKENS), 1)
+    hit = position(col, off_ref, head) == row
+    put0 = (hit & (col < 120)).astype(F32).astype(BF16)
+    put1 = (hit & ((col < 112) | (col >= 120))).astype(F32).astype(BF16)
+    four = r4[0]
+    all0 = r0[0, 0].astype(F32) + nn(put0, jnp.concatenate([rbuf[0, 0], four], axis=0))
+    all1 = r0[0, 1].astype(F32) + nn(put1, jnp.concatenate([rbuf[0, 1], four], axis=0))
+    all1 = all1 + jnp.where(upper == 0, r0b[0].astype(F32), 0.0)
+    out_ref[...] = all0[:, :DH].astype(BF16)
+    dq_ref[...] = all0[:, DH:].astype(BF16)
+    dk_ref[...] = all1[:, :DH].astype(BF16)
+    dv_ref[...] = all1[:, DH:].astype(BF16)
+    log_ref[...] = lse_ref[...]
+
+
 def on_device(query_in, key_in, value_in, grad_out, offsets):
-    flat = jax.ShapeDtypeStruct((TOKENS, HEADS * DH), BF16)
-    vmem = pl.BlockSpec(memory_space=pltpu.VMEM)
-    return pl.pallas_call(
+    hbm = pl.BlockSpec(memory_space=pl.ANY)
+    smem = pl.BlockSpec(memory_space=pltpu.SMEM)
+    parts = pl.pallas_call(
         kernel,
-        out_shape=(flat, jax.ShapeDtypeStruct((HEADS, TOKENS), F32), flat, flat, flat),
-        in_specs=[pl.BlockSpec(memory_space=pl.ANY)] * 4 + [pl.BlockSpec(memory_space=pltpu.SMEM)],
-        out_specs=(vmem,) * 5,
+        out_shape=(
+            jax.ShapeDtypeStruct((HEADS, TOKENS), F32),
+            jax.ShapeDtypeStruct((HEADS, 2, TOKENS, 256), BF16),
+            jax.ShapeDtypeStruct((HEADS, TOKENS, 256), BF16),
+            jax.ShapeDtypeStruct((HEADS, 2, 112, 256), BF16),
+            jax.ShapeDtypeStruct((HEADS, 16, 256), BF16),
+        ),
+        in_specs=[hbm] * 4 + [smem],
+        out_specs=(pl.BlockSpec(memory_space=pltpu.VMEM),) + (hbm,) * 4,
         scratch_shapes=[
             pltpu.VMEM((HEADS, 2, TOKENS, 256), BF16),
             pltpu.VMEM((HEADS, 2, 112, 256), BF16),
@@ -548,10 +563,6 @@
             pltpu.VMEM((HALF, 256), F32),
             pltpu.VMEM((SLOTS, 2, SUB, 256), BF16),
             pltpu.VMEM((SEQ_DEVICES, 16, 256), BF16),
-            pltpu.VMEM((HEADS, 2, TOKENS, 256), BF16),
-            pltpu.VMEM((HEADS, TOKENS, 256), BF16),
-            pltpu.VMEM((HEADS, 2, 112, 256), BF16),
-            pltpu.VMEM((HEADS, 16, 256), BF16),
             pltpu.SemaphoreType.DMA,
             pltpu.SemaphoreType.DMA((LEVELS * HEADS,)),
             pltpu.SemaphoreType.DMA((HEADS,)),
@@ -569,6 +580,22 @@
             collective_id=0, has_side_effects=True, vmem_limit_bytes=60 * 1024 * 1024
         ),
     )(query_in, key_in, value_in, grad_out, offsets)
+    flat = jax.ShapeDtypeStruct((TOKENS, HEADS * DH), BF16)
+    lanes = pl.BlockSpec((TOKENS, DH), lambda h: (0, h))
+    return pl.pallas_call(
+        finish,
+        grid=(HEADS,),
+        out_shape=(flat, jax.ShapeDtypeStruct((HEADS, TOKENS), F32), flat, flat, flat),
+        in_specs=[
+            smem,
+            pl.BlockSpec((HEADS, TOKENS), lambda h: (0, 0)),
+            pl.BlockSpec((1, 2, TOKENS, 256), lambda h: (h, 0, 0, 0)),
+            pl.BlockSpec((1, TOKENS, 256), lambda h: (h, 0, 0)),
+            pl.BlockSpec((1, 2, 112, 256), lambda h: (h, 0, 0, 0)),
+            pl.BlockSpec((1, 16, 256), lambda h: (h, 0, 0)),
+        ],
+        out_specs=(lanes, pl.BlockSpec((HEADS, TOKENS), lambda h: (0, 0)), lanes, lanes, lanes),
+    )(offsets, *parts)
 
 
 def solution(mesh):

time: 83.2 us -> 80.7 us (0.970)
  local copies, waits for them, and re-layouts: 4.85 us -> 0 us
  Pallas kernels: 77.4 us -> 79.8 us
    unnamed x13 -> x0, local copies, waits for them, and re-layouts: 4.85 us -> none
    pallas_call x1 -> x2, Pallas kernels: 77.4 us -> 79.8 us  [the longest x1 75.4 us: on_device(): pl.pallas_call(kernel, out_shape=(jax.ShapeDtypeStruct((HEADS, TOKENS), F...]
where the time goes in v3:
time: 80.7 us; the launch traced here: 80.4 us
  Pallas kernels  79.8 us (99%)
    pallas_call x1, Pallas kernels, on_device(): pl.pallas_call(kernel, out_shape=(jax.ShapeDtypeStruct((HEADS, TOKENS), F...  75.4 us
    pallas_call x1, Pallas kernels, on_device(): pl.pallas_call(finish, grid=(HEADS,), out_shape=(flat, jax.ShapeDtypeStru...  4.38 us

profile of v3, /device:TPU:31, one launch (start us, length us, event | category | flops | bytes accessed | tf_op | source)
XLA Modules:
  0.0 80.4 jit_solution(4657770521922038177)
XLA Ops:
  0.6 75.4 %shard_map.92 = (f32[5,128]{1,0:T(8,128)}, bf16[5,2,128,256]{3,2,1,0:T(8,128)(2,1)}, bf16[5,128,256]{2,1,0:T(8,128)(2,1)}, bf16[5,2,112,256]{3,2,1,0:T(8,128)(2,1)}, bf16[5,16,256]{2,1,0:T(8,128)(2,1)}) custom-call(bf16[128,640]{1,0:T(8,128)(2,1)} %q_ref.1, bf16[128,640]{1,0:T(8,128)(2,1)} %k_ref.1, bf16[128,640]{1,0:T(8,128)(2,1)} %v_ref.1, ...), custom_call_target="tpu_custom_call" | custom-call | tf_op jit(solution)/shard_map/pallas_call | solution.py:539
  76.0 4.4 %shard_map.93 = (bf16[128,640]{1,0:T(8,128)(2,1)}, f32[5,128]{1,0:T(8,128)}, bf16[128,640]{1,0:T(8,128)(2,1)}, bf16[128,640]{1,0:T(8,128)(2,1)}, bf16[128,640]{1,0:T(8,128)(2,1)}) custom-call(s32[5,5]{1,0:T(8,128)} %off_ref.3, f32[5,128]{1,0:T(8,128)} %get-tuple-element.10.lse_ref, bf16[5,2,128,256]{3,2,1,0:T(8,128)(2,1)} %get-tuple-element.11.r0, ...), custom_call_target="tpu_custom_call" | custom-call | tf_op jit(solution)/shard_map/pallas_call | solution.py:585

commit v4 on v3

--- a/solution.py
+++ b/solution.py
@@ -146,13 +146,42 @@
 
     barrier = pltpu.get_barrier_semaphore()
 
-    def greet(i, carry):
-        pl.semaphore_signal(
-            barrier, inc=1, device_id={"seq": lax.rem(me + 1 + lax.rem(i + 15, 63), SEQ_DEVICES)}, device_id_type=MESH
-        )
-        return carry
-
-    lax.fori_loop(0, SEQ_DEVICES - 1, greet, 0)
+    def greet(target):
+        pl.semaphore_signal(barrier, inc=1, device_id={"seq": target}, device_id_type=MESH)
+
+    def greet_members(count):
+        first = me - lax.rem(me, count)
+
+        def one(i, carry):
+            greet(first + lax.rem(me - first + i, count))
+            return carry
+
+        lax.fori_loop(1, count, one, 0)
+
+    other = me - 2 * upper - core + 2 - 2 * upper
+    greet(start[0] + 1 - core)
+    greet(other)
+    greet(other + 1)
+    greetings = jnp.int32(3)
+    for level in range(LEVELS - 1, 0, -1):
+
+        def greet_holder(head, count):
+            target, _ = holder(level, head)
+
+            @pl.when(target != me)
+            def _():
+                greet(target)
+
+            return count + jnp.where(target != me, 1, 0)
+
+        greetings = lax.fori_loop(0, HEADS, greet_holder, greetings)
+    for level in (level4, level3):
+
+        @pl.when(level > 0)
+        def _():
+            greet_members(4 << level)
+
+        greetings = greetings + jnp.where(level > 0, lax.shift_left(4, jnp.maximum(level, 0)) - 1, 0)
 
     def load(head, carry):
         lanes = pl.ds(pl.multiple_of(head * DH, DH), DH)
@@ -180,7 +209,7 @@
 
     lax.fori_loop(0, HEADS, select, 0)
 
-    pl.semaphore_wait(barrier, SEQ_DEVICES - 1)
+    pl.semaphore_wait(barrier, greetings)
 
     def in_copy(level, head):
         rows = ROWS[level]
@@ -514,23 +543,58 @@
     lax.fori_loop(0, SLOTS, drain, 0)
 
 
-def finish(off_ref, lse_ref, r0, r0b, rbuf, r4, out_ref, log_ref, dq_ref, dk_ref, dv_ref):
-    head = pl.program_id(0)
+def finish(off_ref, lse_ref, r0, r0b, rbuf, r4, out_ref, log_ref, dq_ref, dk_ref, dv_ref, w0, w0b, wbuf, res, log, in_sem, out_sem):
     upper = lax.rem(lax.div(lax.axis_index("seq"), 2), 2)
     row = lax.broadcasted_iota(jnp.int32, (TOKENS, TOKENS), 0)
     col = lax.broadcasted_iota(jnp.int32, (TOKENS, TOKENS), 1)
-    hit = position(col, off_ref, head) == row
-    put0 = (hit & (col < 120)).astype(F32).astype(BF16)
-    put1 = (hit & ((col < 112) | (col >= 120))).astype(F32).astype(BF16)
-    four = r4[0]
-    all0 = r0[0, 0].astype(F32) + nn(put0, jnp.concatenate([rbuf[0, 0], four], axis=0))
-    all1 = r0[0, 1].astype(F32) + nn(put1, jnp.concatenate([rbuf[0, 1], four], axis=0))
-    all1 = all1 + jnp.where(upper == 0, r0b[0].astype(F32), 0.0)
-    out_ref[...] = all0[:, :DH].astype(BF16)
-    dq_ref[...] = all0[:, DH:].astype(BF16)
-    dk_ref[...] = all1[:, :DH].astype(BF16)
-    dv_ref[...] = all1[:, DH:].astype(BF16)
-    log_ref[...] = lse_ref[...]
+
+    def ins(head):
+        return (
+            pltpu.make_async_copy(r0.at[head], w0.at[head], in_sem.at[0, head]),
+            pltpu.make_async_copy(r0b.at[head], w0b.at[head], in_sem.at[1, head]),
+            pltpu.make_async_copy(rbuf.at[head], wbuf.at[head, :, pl.ds(0, 112), :], in_sem.at[2, head]),
+            pltpu.make_async_copy(r4.at[head], wbuf.at[head, 0, pl.ds(112, 16), :], in_sem.at[3, head]),
+            pltpu.make_async_copy(r4.at[head], wbuf.at[head, 1, pl.ds(112, 16), :], in_sem.at[4, head]),
+        )
+
+    def outs(head):
+        lanes = pl.ds(head * DH, DH)
+        return [
+            pltpu.make_async_copy(res.at[n, head], ref.at[:, lanes], out_sem.at[n, head])
+            for n, ref in enumerate((out_ref, dq_ref, dk_ref, dv_ref))
+        ]
+
+    for head in range(HEADS):
+        for copy in ins(head):
+            copy.start()
+    log_in = pltpu.make_async_copy(lse_ref, log, in_sem.at[5, 0])
+    log_out = pltpu.make_async_copy(log, log_ref, out_sem.at[4, 0])
+    log_in.start()
+    puts = []
+    for head in range(HEADS):
+        hit = position(col, off_ref, head) == row
+        puts.append((
+            (hit & (col < 120)).astype(F32).astype(BF16),
+            (hit & ((col < 112) | (col >= 120))).astype(F32).astype(BF16),
+        ))
+    log_in.wait()
+    log_out.start()
+    for head in range(HEADS):
+        for copy in ins(head):
+            copy.wait()
+        all0 = w0[head, 0].astype(F32) + nn(puts[head][0], wbuf[head, 0])
+        all1 = w0[head, 1].astype(F32) + nn(puts[head][1], wbuf[head, 1])
+        all1 = all1 + jnp.where(upper == 0, w0b[head].astype(F32), 0.0)
+        res[0, head] = all0[:, :DH].astype(BF16)
+        res[1, head] = all0[:, DH:].astype(BF16)
+        res[2, head] = all1[:, :DH].astype(BF16)
+        res[3, head] = all1[:, DH:].astype(BF16)
+        for copy in outs(head):
+            copy.start()
+    for head in range(HEADS):
+        for copy in outs(head):
+            copy.wait()
+    log_out.wait()
 
 
 def on_device(query_in, key_in, value_in, grad_out, offsets):
@@ -581,20 +645,21 @@
         ),
     )(query_in, key_in, value_in, grad_out, offsets)
     flat = jax.ShapeDtypeStruct((TOKENS, HEADS * DH), BF16)
-    lanes = pl.BlockSpec((TOKENS, DH), lambda h: (0, h))
     return pl.pallas_call(
         finish,
-        grid=(HEADS,),
         out_shape=(flat, jax.ShapeDtypeStruct((HEADS, TOKENS), F32), flat, flat, flat),
-        in_specs=[
-            smem,
-            pl.BlockSpec((HEADS, TOKENS), lambda h: (0, 0)),
-            pl.BlockSpec((1, 2, TOKENS, 256), lambda h: (h, 0, 0, 0)),
-            pl.BlockSpec((1, TOKENS, 256), lambda h: (h, 0, 0)),
-            pl.BlockSpec((1, 2, 112, 256), lambda h: (h, 0, 0, 0)),
-            pl.BlockSpec((1, 16, 256), lambda h: (h, 0, 0)),
+        in_specs=[smem] + [hbm] * 5,
+        out_specs=(hbm,) * 5,
+        scratch_shapes=[
+            pltpu.VMEM((HEADS, 2, TOKENS, 256), BF16),
+            pltpu.VMEM((HEADS, TOKENS, 256), BF16),
+            pltpu.VMEM((HEADS, 2, TOKENS, 256), BF16),
+            pltpu.VMEM((4, HEADS, TOKENS, DH), BF16),
+            pltpu.VMEM((HEADS, TOKENS), F32),
+            pltpu.SemaphoreType.DMA((6, HEADS)),
+            pltpu.SemaphoreType.DMA((5, HEADS)),
         ],
-        out_specs=(lanes, pl.BlockSpec((HEADS, TOKENS), lambda h: (0, 0)), lanes, lanes, lanes),
+        compiler_params=pltpu.CompilerParams(vmem_limit_bytes=60 * 1024 * 1024),
     )(offsets, *parts)
 
 

time: 80.7 us -> 79 us (0.979)
  the two profiles are of different devices: /device:TPU:31 before, /device:TPU:1 now
where the time goes in v4:
time: 79 us; the launch traced here: 78 us
  Pallas kernels  77.3 us (98%)
    pallas_call x1, Pallas kernels, on_device(): pl.pallas_call(kernel, out_shape=(jax.ShapeDtypeStruct((HEADS, TOKENS), F...  73.2 us
    pallas_call x1, Pallas kernels, on_device(): pl.pallas_call(finish, out_shape=(flat, jax.ShapeDtypeStruct((HEADS, TOKE...  4.08 us

profile of v4, /device:TPU:1, one launch (start us, length us, event | category | flops | bytes accessed | tf_op | source)
XLA Modules:
  0.0 78.0 jit_solution(12934454643833872027)
XLA Ops:
  0.6 73.2 %shard_map.92 = (f32[5,128]{1,0:T(8,128)}, bf16[5,2,128,256]{3,2,1,0:T(8,128)(2,1)}, bf16[5,128,256]{2,1,0:T(8,128)(2,1)}, bf16[5,2,112,256]{3,2,1,0:T(8,128)(2,1)}, bf16[5,16,256]{2,1,0:T(8,128)(2,1)}) custom-call(bf16[128,640]{1,0:T(8,128)(2,1)} %q_ref.1, bf16[128,640]{1,0:T(8,128)(2,1)} %k_ref.1, bf16[128,640]{1,0:T(8,128)(2,1)} %v_ref.1, ...), custom_call_target="tpu_custom_call" | custom-call | tf_op jit(solution)/shard_map/pallas_call | solution.py:603
  73.9 4.1 %shard_map.93 = (bf16[128,640]{1,0:T(8,128)(2,1)}, f32[5,128]{1,0:T(8,128)}, bf16[128,640]{1,0:T(8,128)(2,1)}, bf16[128,640]{1,0:T(8,128)(2,1)}, bf16[128,640]{1,0:T(8,128)(2,1)}) custom-call(s32[5,5]{1,0:T(8,128)} %off_ref.3, f32[5,128]{1,0:T(8,128)} %get-tuple-element.10.lse_ref, bf16[5,2,128,256]{3,2,1,0:T(8,128)(2,1)} %get-tuple-element.11.r0, ...), custom_call_target="tpu_custom_call" | custom-call | tf_op jit(solution)/shard_map/pallas_call | solution.py:648

commit v5 on v4

--- a/solution.py
+++ b/solution.py
@@ -233,7 +233,7 @@
         at = pl.ds(pl.multiple_of(core * TOKENS, TOKENS), TOKENS)
         return s0.at[head, 1], ubuf.at[slot, 1, at, :], target + 2, kv_send.at[head], kv_recv.at[slot]
 
-    turn = lax.div(me, 2)
+    turn = me
     for level in range(LEVELS - 1, -1, -1):
 
         def send_rows(i, carry):

time: 79 us -> 78 us (0.987)
  no operation moved by 1% of the time
where the time goes in v5:
time: 78 us; the launch traced here: 77.7 us
  Pallas kernels  77 us (99%)
    pallas_call x1, Pallas kernels, on_device(): pl.pallas_call(kernel, out_shape=(jax.ShapeDtypeStruct((HEADS, TOKENS), F...  73 us
    pallas_call x1, Pallas kernels, on_device(): pl.pallas_call(finish, out_shape=(flat, jax.ShapeDtypeStruct((HEADS, TOKE...  4.08 us

profile of v5, /device:TPU:1, one launch (start us, length us, event | category | flops | bytes accessed | tf_op | source)
XLA Modules:
  0.0 77.7 jit_solution(6991716662995686473)
XLA Ops:
  0.6 73.0 %shard_map.92 = (f32[5,128]{1,0:T(8,128)}, bf16[5,2,128,256]{3,2,1,0:T(8,128)(2,1)}, bf16[5,128,256]{2,1,0:T(8,128)(2,1)}, bf16[5,2,112,256]{3,2,1,0:T(8,128)(2,1)}, bf16[5,16,256]{2,1,0:T(8,128)(2,1)}) custom-call(bf16[128,640]{1,0:T(8,128)(2,1)} %q_ref.1, bf16[128,640]{1,0:T(8,128)(2,1)} %k_ref.1, bf16[128,640]{1,0:T(8,128)(2,1)} %v_ref.1, ...), custom_call_target="tpu_custom_call" | custom-call | tf_op jit(solution)/shard_map/pallas_call | solution.py:603
  73.6 4.1 %shard_map.93 = (bf16[128,640]{1,0:T(8,128)(2,1)}, f32[5,128]{1,0:T(8,128)}, bf16[128,640]{1,0:T(8,128)(2,1)}, bf16[128,640]{1,0:T(8,128)(2,1)}, bf16[128,640]{1,0:T(8,128)(2,1)}) custom-call(s32[5,5]{1,0:T(8,128)} %off_ref.3, f32[5,128]{1,0:T(8,128)} %get-tuple-element.10.lse_ref, bf16[5,2,128,256]{3,2,1,0:T(8,128)(2,1)} %get-tuple-element.11.r0, ...), custom_call_target="tpu_custom_call" | custom-call | tf_op jit(solution)/shard_map/pallas_call | solution.py:648

commit v6 on v5

--- a/solution.py
+++ b/solution.py
@@ -493,14 +493,6 @@
 
     lax.fori_loop(0, SLOTS, backward, 0)
 
-    arrived(r4, res_recv.at[2])
-    arrived(rbuf, res_recv.at[1])
-    arrived(r0, res_recv.at[0])
-
-    @pl.when(upper == 0)
-    def _():
-        arrived(r0b, res_recv.at[3])
-
     def drain_own(head, carry):
         for level in range(LEVELS):
             src, _, target, sem, _ = in_copy(level, head)
@@ -541,6 +533,14 @@
         return carry
 
     lax.fori_loop(0, SLOTS, drain, 0)
+
+    arrived(r4, res_recv.at[2])
+    arrived(rbuf, res_recv.at[1])
+    arrived(r0, res_recv.at[0])
+
+    @pl.when(upper == 0)
+    def _():
+        arrived(r0b, res_recv.at[3])
 
 
 def finish(off_ref, lse_ref, r0, r0b, rbuf, r4, out_ref, log_ref, dq_ref, dk_ref, dv_ref, w0, w0b, wbuf, res, log, in_sem, out_sem):

time: 78 us -> 76.9 us (0.986)
  Pallas kernels: 77 us -> 76 us
    pallas_call x1, Pallas kernels: 73 us -> 71.9 us  [on_device(): pl.pallas_call(kernel, out_shape=(jax.ShapeDtypeStruct((HEADS, TOKENS), F...]
where the time goes in v6:
time: 76.9 us; the launch traced here: 76.6 us
  Pallas kernels  76 us (99%)
    pallas_call x1, Pallas kernels, on_device(): pl.pallas_call(kernel, out_shape=(jax.ShapeDtypeStruct((HEADS, TOKENS), F...  71.9 us
    pallas_call x1, Pallas kernels, on_device(): pl.pallas_call(finish, out_shape=(flat, jax.ShapeDtypeStruct((HEADS, TOKE...  4.08 us

profile of v6, /device:TPU:1, one launch (start us, length us, event | category | flops | bytes accessed | tf_op | source)
XLA Modules:
  0.0 76.6 jit_solution(14836236751316044256)
XLA Ops:
  0.6 71.9 %shard_map.92 = (f32[5,128]{1,0:T(8,128)}, bf16[5,2,128,256]{3,2,1,0:T(8,128)(2,1)}, bf16[5,128,256]{2,1,0:T(8,128)(2,1)}, bf16[5,2,112,256]{3,2,1,0:T(8,128)(2,1)}, bf16[5,16,256]{2,1,0:T(8,128)(2,1)}) custom-call(bf16[128,640]{1,0:T(8,128)(2,1)} %q_ref.1, bf16[128,640]{1,0:T(8,128)(2,1)} %k_ref.1, bf16[128,640]{1,0:T(8,128)(2,1)} %v_ref.1, ...), custom_call_target="tpu_custom_call" | custom-call | tf_op jit(solution)/shard_map/pallas_call | solution.py:603
  72.5 4.1 %shard_map.93 = (bf16[128,640]{1,0:T(8,128)(2,1)}, f32[5,128]{1,0:T(8,128)}, bf16[128,640]{1,0:T(8,128)(2,1)}, bf16[128,640]{1,0:T(8,128)(2,1)}, bf16[128,640]{1,0:T(8,128)(2,1)}) custom-call(s32[5,5]{1,0:T(8,128)} %off_ref.3, f32[5,128]{1,0:T(8,128)} %get-tuple-element.10.lse_ref, bf16[5,2,128,256]{3,2,1,0:T(8,128)(2,1)} %get-tuple-element.11.r0, ...), custom_call_target="tpu_custom_call" | custom-call | tf_op jit(solution)/shard_map/pallas_call | solution.py:648
